TPU v7x, 32 devices: a whole 2x2x4 slice. The times are simulated.
32 devices in a mesh: seq: 4 (over y, x), grp: 8 (over z, core).
Axes of the slice: x: 2, y: 2, z: 4, core: 2. Of those that a mesh axis runs over, the one named last changes fastest.
Arguments:
- p_x: bfloat16 [8, 1024, 2048], P('grp', 'seq'), may hold values from -6 to 6
- p_bc: bfloat16 [8, 1024, 256], P('grp', 'seq'), may hold values from -4 to 4
- p_dt: float32 [8, 32, 1024], P('grp', None, 'seq'), may hold values from 0.005 to 0.04
- p_decay: float32 [8, 32, 1024], P('grp', None, 'seq'), may hold values from -1 to 0
- r_x: bfloat16 [16384, 2048], P('grp', 'seq'), may hold values from -6 to 6
- r_bc: bfloat16 [16384, 256], P('grp'), may hold values from -4 to 4
- r_dt: float32 [32, 16384], P('seq', 'grp'), may hold values from 0.005 to 0.04
- r_decay: float32 [32, 16384], P('seq', 'grp'), may hold values from -1 to 0
- pack_list: int32 [8, 8], P('grp'), may hold values from -1 to 47, as said below
- resp_len: int32 [48], replicated, may hold values from 32 to 256, as said below
- resp_prompt: int32 [48], replicated, may hold values from 0 to 7, as said below
- d_skip: float32 [32], replicated, may hold values from 0.5 to 1.5
Outputs:
- p_out: bfloat16 [8, 1024, 2048], P('grp', 'seq')
- r_out: bfloat16 [16384, 2048], P('grp', 'seq')
Inputs may be any that keep to these rules, and one draw needn't show every extreme that they name: `pack_list`: row g lists the responses placed on index g of grp in the order of their rows, -1 marking an empty slot; every response stands in exactly one slot. `resp_len`: a device's responses take its rows one after another from its first row in slot order; the rows after them are unused. `resp_prompt`: every prompt has exactly 6 responses.
All inputs are finite; a program needn't handle non-finite values.
Results may differ from a plain program's by a relative error of at most 0.0053.
Values may be sent and summed in bfloat16 or wider, within the bound.
A program may use at most 64 MiB of HBM per device.

v0:
```python
import jax
import jax.numpy as jnp
from jax import lax
from jax.sharding import PartitionSpec as P

STRETCH = 256


def carried_in(value, axis, join, neutral):
    count, mine = (lax.axis_size(axis), lax.axis_index(axis))
    pieces = jax.tree.map(lambda part: lax.all_gather(part, axis), value)
    total = jax.tree.map(
        lambda part, zero: jnp.full_like(part, 0) + jnp.asarray(zero, part.dtype), value, neutral
    )

    def turn(position, total):
        longer = join(total, jax.tree.map(lambda part: part[position], pieces))
        return jax.tree.map(lambda new, old: jnp.where(position < mine, new, old), longer, total)

    return lax.fori_loop(0, count - 1, turn, total)


def from_root(value, axis, source):
    kept = jnp.where(lax.axis_index(axis) == source, value, 0).astype(value.dtype)
    return lax.psum(kept, axis)


def product(einsum_form, left_side, right_side):
    return jnp.einsum(einsum_form, left_side, right_side, preferred_element_type=jnp.float32)


def block_terms(block_x, block_bc, block_dt, block_decay, block_slot):
    length = block_x.shape[0]
    head_count = block_dt.shape[0]
    state_width = block_bc.shape[1] // 2
    inputs = block_x.reshape(length, head_count, -1)
    b_rows = block_bc[:, :state_width]
    c_rows = block_bc[:, state_width:]
    running = jnp.cumsum(block_decay, axis=1)
    before = running - block_decay
    places = jnp.arange(length)
    same_span = (block_slot[:, None] == block_slot[None, :]) & (places[None, :] <= places[:, None])
    starts_here = jnp.concatenate([jnp.ones((1,), jnp.bool_), block_slot[1:] != block_slot[:-1]])
    leader = same_span & starts_here[None, :]
    offset = jnp.sum(jnp.where(leader[None], before[:, None, :], 0.0), axis=2)
    gained = running - offset
    scores = jnp.dot(c_rows, b_rows.T, preferred_element_type=jnp.float32)
    spread = jnp.where(same_span[None], running[:, :, None] - running[:, None, :], -jnp.inf)
    mixing = (jnp.exp(spread) * block_dt[:, None, :] * scores[None]).astype(jnp.bfloat16)
    inner_part = product("hij,jhp->ihp", mixing, inputs)
    tail_rows = block_slot == block_slot[length - 1]
    to_end = jnp.where(tail_rows[None], jnp.exp(running[:, length - 1 :] - running) * block_dt, 0.0)
    scaled = (to_end[:, :, None] * b_rows[None].astype(jnp.float32)).astype(jnp.bfloat16)
    local_state = product("hjn,jhp->hnp", scaled, inputs)
    return (inputs, inner_part, gained, local_state, c_rows)


def response_layer(skip_gain, rows_x, rows_bc, rows_dt, rows_decay, row_slot, slot_seeds):
    slot_count = slot_seeds.shape[0]
    blocks = rows_x.shape[0] // STRETCH
    head_count = rows_dt.shape[0]
    sliced = (
        rows_x.reshape(blocks, STRETCH, -1),
        rows_bc.reshape(blocks, STRETCH, -1),
        rows_dt.reshape(head_count, blocks, STRETCH).transpose(1, 0, 2),
        rows_decay.reshape(head_count, blocks, STRETCH).transpose(1, 0, 2),
        row_slot.reshape(blocks, STRETCH),
    )
    slot_ids = jnp.arange(slot_count)

    def advance(carry_pair, pieces):
        carried_state, previous = carry_pair
        block_slot = pieces[4]
        inputs, inner_part, gained, local_state, c_rows = block_terms(
            pieces[0], pieces[1], pieces[2], pieces[3], block_slot
        )
        first_slot = block_slot[0]
        carried_on = first_slot == previous
        chosen = (slot_ids == first_slot) & carried_on
        bases_table = jnp.where(
            chosen[:, None, None, None], carried_state.astype(jnp.bfloat16)[None], slot_seeds
        )
        projected = product("in,khnp->ikhp", c_rows, bases_table)
        hot_rows = (block_slot[:, None] == slot_ids[None, :]).astype(jnp.float32)
        carried = (
            jnp.sum(projected * hot_rows[:, :, None, None], axis=1) * jnp.exp(gained).T[:, :, None]
        )
        output = inner_part + carried + skip_gain[None, :, None] * inputs.astype(jnp.float32)
        output = jnp.where((block_slot < slot_count)[:, None, None], output, 0.0)
        final_slot = block_slot[STRETCH - 1]
        fresh_seed = jnp.sum(
            jnp.where(
                (slot_ids == final_slot)[:, None, None, None], slot_seeds.astype(jnp.float32), 0.0
            ),
            axis=0,
        )
        anchor = jnp.where((final_slot == first_slot) & carried_on, carried_state, fresh_seed)
        carried_state = jnp.exp(gained[:, -1])[:, None, None] * anchor + local_state
        return ((carried_state, final_slot), output.reshape(STRETCH, -1).astype(jnp.bfloat16))

    initial = (jnp.zeros(slot_seeds.shape[1:], jnp.float32), jnp.int32(-1))
    final_pair, outputs = lax.scan(advance, initial, sliced)
    return outputs.reshape(rows_x.shape)


def slot_layout(pack_row, resp_len, resp_prompt, row_count):
    hit_table = pack_row[:, None] == jnp.arange(resp_len.shape[0])[None, :]
    slot_spans = jnp.sum(jnp.where(hit_table, resp_len[None, :], 0), axis=1)
    owners = jnp.where(
        pack_row >= 0, jnp.sum(jnp.where(hit_table, resp_prompt[None, :], 0), axis=1), -1
    )
    limits = jnp.cumsum(slot_spans)
    row_slot = jnp.sum(
        (jnp.arange(row_count)[:, None] >= limits[None, :]).astype(jnp.int32), axis=1
    )
    return (row_slot, owners)


def combine(earlier, later_part):
    return (earlier[0] * later_part[0], later_part[0][:, None, None] * earlier[1] + later_part[1])


def on_device(
    p_x, p_bc, p_dt, p_decay, r_x, r_bc, r_dt, r_decay, pack_list, resp_len, resp_prompt, d_skip
):
    head_count = p_dt.shape[1]
    groups = lax.axis_size("seq")
    block_heads = head_count // groups
    state_width = p_bc.shape[2] // 2
    channels = p_x.shape[2] // head_count
    pieces_list = block_terms(
        p_x[0, 0:STRETCH],
        p_bc[0, 0:STRETCH],
        p_dt[0, :, 0:STRETCH],
        p_decay[0, :, 0:STRETCH],
        jnp.zeros((STRETCH,), jnp.int32),
    )
    local_end = jnp.zeros((head_count, state_width, channels), jnp.float32)
    local_end = jnp.exp(pieces_list[2][:, -1])[:, None, None] * local_end + pieces_list[3]
    decay_total = jnp.exp(jnp.sum(p_decay[0], axis=1))
    ahead_pair = carried_in(
        (decay_total, local_end),
        "seq",
        combine,
        (jnp.ones_like(decay_total), jnp.zeros_like(local_end)),
    )
    prefix = ahead_pair[1]
    whole_state = combine(ahead_pair, (decay_total, local_end))[1]
    final_state = from_root(whole_state.astype(jnp.bfloat16), "seq", groups - 1)
    own_seed = lax.dynamic_slice_in_dim(
        final_state, lax.axis_index("seq") * block_heads, block_heads, 0
    )
    inputs, inner_part, gained, local_state, c_rows = pieces_list
    carried = (
        product("in,hnp->ihp", c_rows, prefix.astype(jnp.bfloat16)) * jnp.exp(gained).T[:, :, None]
    )
    output = inner_part + carried + d_skip[None, :, None] * inputs.astype(jnp.float32)
    outputs = output.reshape(STRETCH, -1).astype(jnp.bfloat16)
    p_out = outputs[None]
    row_slot, owners = slot_layout(pack_list[0], resp_len, resp_prompt, r_x.shape[0])
    gathered_piece = lax.all_gather(own_seed[None], "grp", axis=0, tiled=True)
    chosen = (owners[:, None] == jnp.arange(gathered_piece.shape[0])[None, :]).astype(jnp.bfloat16)
    slot_seeds = product("km,mhnp->khnp", chosen, gathered_piece).astype(jnp.bfloat16)
    skip_block = lax.dynamic_slice_in_dim(
        d_skip, lax.axis_index("seq") * block_heads, block_heads, 0
    )
    r_out = response_layer(skip_block, r_x, r_bc, r_dt, r_decay, row_slot, slot_seeds)
    return (p_out, r_out)


def solution(mesh):
    placed = (
        P("grp", "seq", None),
        P("grp", "seq", None),
        P("grp", None, "seq"),
        P("grp", None, "seq"),
        P("grp", "seq"),
        P("grp", None),
        P("seq", "grp"),
        P("seq", "grp"),
        P("grp", None),
        P(),
        P(),
        P(),
    )
    return jax.shard_map(
        on_device,
        mesh=mesh,
        in_specs=placed,
        out_specs=(P("grp", "seq", None), P("grp", "seq")),
        check_vma=False,
    )
```

profile of v0, /device:TPU:0, one launch (start us, length us, event | category | flops | bytes accessed | tf_op | source)
XLA Modules:
  0.0 289.5 jit_solution(2753412943721960229)
XLA Ops:
  7.2 0.8 reshape.474
  8.9 0.9 bitcast_subtract_fusion.1
  10.6 1.2 select_reduce_fusion.2
  11.8 1.4 exponential_bitcast_fusion.1
  13.4 0.9 slice_convert_fusion.1
  14.3 1.5 copy.76
  15.8 2.5 fusion.40
  19.9 11.3 %all-reduce = f32[128]{0:T(128)S(1)} all-reduce(f32[128]{0:T(128)S(1)} %get-tuple-element.411), channel_id=2, replica_groups=mesh['seq'=4,'grp'=8] {'seq'}, use_global_device_ids=true, to_apply=%add | all-reduce | flops 128 | bytes 1024
  31.3 42.6 %all-gather.6.cloned.1.call-done = f32[128,128,64]{1,2,0:T(8,128)} async-done(((f32[32,128,64]{1,2,0:T(8,128)}), f32[128,128,64]{1,2,0:T(8,128)}) %all-gather.6.cloned.1.call-update) | async-done | bytes 4194320 | tf_op jit(solution)/shard_map/all_gather | solution.py:11
  73.9 14.0 %while.30 = (s32[]{:T(128)}, f32[32,128,64]{2,1,0:T(8,128)}, s32[]{:T(128)}, f32[4,32]{1,0:T(4,128)S(1)}, f32[4,32,128,64]{2,3,1,0:T(8,128)}, /*index=5*/s32[]{:T(128)}, s32[]{:T(128)}) while((s32[]{:T(128)}, f32[32,128,64]{2,1,0:T(8,128)}, s32[]{:T(128)}, f32[4,32]{1,0:T(4,128)S(1)}, f32[4,32,128,64]{2,3,1,0:T(8,128)}, ...), condition=%wide.region_5.6_spmd.clone, body=%wide.region_4.5_spmd.clone.sunk | while | flops 1048580 | bytes 7340521 | solution.py:20
  73.9 1.3 constant_dynamic-slice_fusion.10
  75.8 1.7 fusion.75
  77.5 1.3 constant_dynamic-slice_fusion.10
  79.4 3.3 %fusion.75 = f32[32,128,64]{2,1,0:T(8,128)} fusion(f32[1,32,128,64]{3,2,1,0:T(8,128)S(1)} %copy.106, f32[32,128,64]{2,1,0:T(8,128)} %get-tuple-element.542, f32[32]{0:T(128)S(1)} %dynamic-slice_bitcast_fusion.8, pred[]{:T(512)S(6)} %compare.6, pred[]{:T(512)S(6)} %lt.44), kind=kLoop, calls=%fused_computation.2.clone.1 | loop fusion | flops 1048576 | bytes 3145858 | tf_op jit(solution)/shard_map/while/body/eval_jaxpr/jit(_where)/select_n | solution.py:18
  82.7 1.3 constant_dynamic-slice_fusion.10
  84.6 3.3 %fusion.75 = f32[32,128,64]{2,1,0:T(8,128)} fusion(f32[1,32,128,64]{3,2,1,0:T(8,128)S(1)} %copy.106, f32[32,128,64]{2,1,0:T(8,128)} %get-tuple-element.542, f32[32]{0:T(128)S(1)} %dynamic-slice_bitcast_fusion.8, pred[]{:T(512)S(6)} %compare.6, pred[]{:T(512)S(6)} %lt.44), kind=kLoop, calls=%fused_computation.2.clone.1 | loop fusion | flops 1048576 | bytes 3145858 | tf_op jit(solution)/shard_map/while/body/eval_jaxpr/jit(_where)/select_n | solution.py:18
  87.9 2.2 copy.79
  90.1 2.4 fusion.44
  92.6 45.4 %all-reduce.3.cloned.1.call-done = bf16[32,128,64]{1,2,0:T(8,128)(2,1)} async-done(((bf16[32,128,64]{1,2,0:T(8,128)(2,1)}), bf16[32,128,64]{1,2,0:T(8,128)(2,1)}) %all-reduce.3.cloned.1.call-update) | async-done | bytes 524304 | tf_op jit(solution)/shard_map/psum | solution.py:25
  138.0 1.6 constant_dynamic-slice_fusion.5
  142.3 3.1 %fusion.37 = bf16[256,32,64]{0,2,1:T(8,128)(2,1)S(1)} fusion(f32[32,64,256]{2,1,0:T(8,128)S(1)} %fusion.42, bf16[256,32,64]{0,2,1:T(8,128)(2,1)S(1)} %bitcast.137, f32[256,256]{1,0:T(8,128)S(1)} %fusion.46, f32[32,256]{1,0:T(8,128)S(1)} %bitcast.148, f32[32,256]{1,0:T(8,128)S(1)} %copy-done.6, pred[256,256]{1,0:T(8,128)(4,1)S(1)} %iota_compare_fusion.3, ...), kind=kOutput, calls=%fused_computation.76 | convolution fusion | flops 282066944 | bytes 4620416 | tf_op jit(solution)/shard_map/hij,jhp->ihp/dot_general | solution.py:29
  145.4 1.4 copy.84
  146.9 15.0 %all-gather.8.cloned.1.call-done = bf16[64,128,64]{1,2,0:T(8,128)(2,1)} async-done(((bf16[8,128,64]{1,2,0:T(8,128)(2,1)}), bf16[64,128,64]{1,2,0:T(8,128)(2,1)}) %all-gather.8.cloned.1.call-update) | async-done | bytes 1048592 | tf_op jit(solution)/shard_map/all_gather | solution.py:161
  161.9 2.0 convolution_convert_fusion
  164.1 118.9 %while.31 = (s32[]{:T(128)}, f32[8,128,64]{1,2,0:T(8,128)S(1)}, s32[]{:T(128)}, bf16[8,256,512]{2,1,0:T(8,128)(2,1)}, f32[8,8,256]{2,1,0:T(8,128)}, /*index=5*/s...) while((s32[]{:T(128)}, f32[8,128,64]{1,2,0:T(8,128)S(1)}, ...), condition=%wide.region_17.18_spmd.clone.clone, body=%wide.region_11.17_spmd.clone.clone.sunk | while | flops 395883584 | bytes 9374714 | solution.py:102
  166.7 0.9 dynamic-slice_bitcast_fusion.9
  167.7 0.8 multiply_reduce_fusion.2
  170.3 0.8 bitcast_subtract_fusion.3
  171.6 0.8 exponential_bitcast_fusion.3
  172.6 1.0 constant_dynamic-slice_fusion.11
  181.6 0.9 dynamic-slice_bitcast_fusion.9
  182.6 0.8 multiply_reduce_fusion.2
  185.2 0.8 bitcast_subtract_fusion.3
  187.5 1.0 constant_dynamic-slice_fusion.11
  196.5 0.9 dynamic-slice_bitcast_fusion.9
  197.4 0.8 multiply_reduce_fusion.2
  200.0 0.8 bitcast_subtract_fusion.3
  201.3 0.8 exponential_bitcast_fusion.3
  202.3 1.0 constant_dynamic-slice_fusion.11
  211.3 0.9 dynamic-slice_bitcast_fusion.9
  212.3 0.8 multiply_reduce_fusion.2
  214.9 0.8 bitcast_subtract_fusion.3
  216.2 0.8 exponential_bitcast_fusion.3
  217.2 1.0 constant_dynamic-slice_fusion.11
  226.2 0.9 dynamic-slice_bitcast_fusion.9
  227.2 0.8 multiply_reduce_fusion.2
  229.7 0.8 bitcast_subtract_fusion.3
  231.1 0.8 exponential_bitcast_fusion.3
  232.0 1.0 constant_dynamic-slice_fusion.11
  241.1 0.9 dynamic-slice_bitcast_fusion.9
  242.0 0.8 multiply_reduce_fusion.2
  244.6 0.8 bitcast_subtract_fusion.3
  245.9 0.8 exponential_bitcast_fusion.3
  246.9 1.0 constant_dynamic-slice_fusion.11
  255.9 0.9 dynamic-slice_bitcast_fusion.9
  256.9 0.8 multiply_reduce_fusion.2
  259.5 0.8 bitcast_subtract_fusion.3
  260.8 0.8 exponential_bitcast_fusion.3
  261.8 1.0 constant_dynamic-slice_fusion.11
  270.8 0.9 dynamic-slice_bitcast_fusion.9
  271.7 0.8 multiply_reduce_fusion.2
  274.3 0.8 bitcast_subtract_fusion.3
  275.7 0.8 exponential_bitcast_fusion.3
  276.6 1.0 constant_dynamic-slice_fusion.11
  (276 shorter events, 71.4 us)
Async XLA Ops:
  7.2 66.7 %all-gather.6.cloned.1.call-start = ((), (), s32[]{:S(2)}) async-start(), calls=%async_computation.1 | async-start | bytes 5242880 | tf_op jit(solution)/shard_map/all_gather | solution.py:11
  8.9 1.0 copy-start.5
  15.8 58.1 %copy-start.1 = (bf16[1,256,2048]{1,2,0:T(8,128)(2,1)}, bf16[1,256,2048]{1,2,0:T(8,128)(2,1)S(1)}, u32[]{:S(2)}) copy-start(bf16[1,256,2048]{1,2,0:T(8,128)(2,1)S(1)} %copy.76) | copy-start | bytes 3145732
  15.8 2.6 copy-start.4
  15.8 2.7 copy-start.13
  18.3 119.7 %all-reduce.3.cloned.1.call-start = ((), (), s32[]{:S(2)}) async-start(), calls=%async_computation | async-start | bytes 1048576 | tf_op jit(solution)/shard_map/psum | solution.py:25
  90.1 50.3 %copy-start.9 = (s32[48]{0:T(128)S(1)}, s32[48]{0:T(128)}, u32[]{:S(2)}) copy-start(s32[48]{0:T(128)} %param.26) | copy-start | bytes 580
  90.1 50.3 %copy-start.10 = (s32[48]{0:T(128)S(1)}, s32[48]{0:T(128)}, u32[]{:S(2)}) copy-start(s32[48]{0:T(128)} %param.25) | copy-start | bytes 580
  90.1 50.3 %copy-start.11 = (s32[1,8]{1,0:T(1,128)S(1)}, s32[1,8]{1,0:T(1,128)}, u32[]{:S(2)}) copy-start(s32[1,8]{1,0:T(1,128)} %param.24) | copy-start | bytes 100
  90.1 50.8 %copy-start.3 = (bf16[1,256,256]{2,1,0:T(8,128)(2,1)S(1)}, bf16[1,256,256]{2,1,0:T(8,128)(2,1)}, u32[]{:S(2)}) copy-start(bf16[1,256,256]{2,1,0:T(8,128)(2,1)} %param.17) | copy-start | bytes 393220
  90.1 51.0 %copy-start = (f32[32,128,64]{2,1,0:T(8,128)S(1)}, f32[32,128,64]{2,1,0:T(8,128)}, u32[]{:S(2)}) copy-start(f32[32,128,64]{2,1,0:T(8,128)} %get-tuple-element.164) | copy-start | bytes 3145732
  92.5 69.3 %all-gather.8.cloned.1.call-start = ((), (), s32[]{:S(2)}) async-start(), calls=%async_computation.2 | async-start | bytes 1179648 | tf_op jit(solution)/shard_map/all_gather | solution.py:161
  141.1 1.2 copy-start.2
  141.1 1.2 copy-start.6
  141.1 1.2 copy-start.7
  141.1 1.2 copy-start.8
  141.1 1.2 copy-start.12
Sparse Core Ops, SparseCore 0:
  18.4 55.4 all-gather.5
  92.6 45.3 all-reduce.2
  139.7 22.0 all-gather.7
where the time goes:
time: 292 us; the launch traced here: 290 us
  waiting for transfers between devices  103 us (35%)
  other arithmetic  57.7 us (20%)
  local copies, waits for them, and re-layouts  53.9 us (18%)
  matrix products  26.4 us (9%)
  loops' own time  22.2 us (8%)
  between operations  14.7 us (5%)
  blocking collectives  11.3 us (4%)
    psum x1, waiting for transfers between devices, from_root(): return lax.psum(kept, axis)  45.4 us
    all_gather x1, waiting for transfers between devices, carried_in(): pieces = jax.tree.map(lambda part: lax.all_gather(part, axis), value)  42.6 us
    dot_general x28, matrix products, product(): jnp.einsum(einsum_form, left_side, right_side, preferred_element_type=jnp...  24.8 us
    another operation x1, loops' own time, response_layer(): final_pair, outputs = lax.scan(advance, initial, sliced)  22.1 us
    all_gather x1, waiting for transfers between devices, on_device(): gathered_piece = lax.all_gather(own_seed[None], 'grp', axis=0, tiled=True)  15 us
    unnamed x1, blocking collectives  11.3 us
    dynamic_slice x16, local copies, waits for them, and re-layouts, response_layer(): final_pair, outputs = lax.scan(advance, initial, sliced)  8.85 us
    select_n x3, other arithmetic, turn(): jnp.where(position < mine, new, old)  8.18 us
  transfers between devices with their start and end apart: 3, of which 3 were waited for; matrix products, arithmetic and copies ran while one was open for 3% of the time, Pallas kernels for 0%

commit v1 on v0

v1 whole, which is shorter than its diff:
```python
import functools

import jax
import jax.numpy as jnp
from jax import lax
from jax.experimental import pallas as pl
from jax.experimental.pallas import tpu as pltpu
from jax.sharding import PartitionSpec as P

TILE = 128
STATE = 128
CHANNELS = 64
LOG2E = 1.4426950408889634
F32 = jnp.float32
BF16 = jnp.bfloat16
MESH = pl.DeviceIdType.MESH


def dot(a, b):
    return jnp.dot(a, b, preferred_element_type=F32)


def dot_nt(a, b):
    return lax.dot_general(a, b, (((1,), (1,)), ((), ())), preferred_element_type=F32)


def dot_tn(a, b):
    return lax.dot_general(a, b, (((0,), (0,)), ((), ())), preferred_element_type=F32)


def split(value, terms):
    parts = []
    for _ in range(terms):
        part = value.astype(BF16).astype(F32)
        parts.append(part)
        value = value - part
    return parts


def iota(shape, dim):
    return lax.broadcasted_iota(jnp.int32, shape, dim)


def spreader(rows, columns, bases):
    row = iota((rows, columns), 0)
    head = iota((rows, columns), 1) >> 6
    hit = row == head + bases[0]
    for base in bases[1:]:
        hit = hit | (row == head + base)
    return jnp.where(hit, 1.0, 0.0).astype(BF16)


def paired(x_pair):
    first = iota(x_pair.shape, 1) < CHANNELS
    wide = x_pair.astype(F32)
    return jnp.concatenate([jnp.where(first, wide, 0.0), jnp.where(first, 0.0, wide)], axis=0).astype(BF16)


def diagonal(column, row, bias, scores, x_tile, heads):
    pieces = []
    for pair in range(heads // 2):
        mixes = []
        for h in (2 * pair, 2 * pair + 1):
            power = column[:, h : h + 1] + (row[h : h + 1, :] + bias)
            mixes.append((jnp.exp2(power) * scores).astype(BF16))
        x_pair = x_tile[:, pair * 2 * CHANNELS : (pair + 1) * 2 * CHANNELS]
        pieces.append(dot(jnp.concatenate(mixes, axis=1), paired(x_pair)))
    return pieces


def kernel(
    sizes,
    px_hbm, pbc_hbm, pdt_ref, pdec_ref, rx_hbm, rbc_hbm, rdt_ref, rdec_ref, pack_ref, len_ref, prm_ref, d_ref,
    pout_hbm, rout_hbm,
    px, pbc, rx, rbc, pv, pt, pe, ptot, pacc, dwide, rv, rt, re, rtot, racc, rdecs,
    abuf, arecv, pbuf, precv, seeds, pout, rout,
    in_sem, out_sem, a_send, a_recv, x_send, x_recv, g_recv, up_send, down_send, tu_send, td_send,
):
    seqs, grps, heads, block_heads, head_rows, slots, tiles = sizes
    cols = heads * CHANNELS
    cb = block_heads * CHANNELS
    me = lax.axis_index("seq")
    g = lax.axis_index("grp")
    z, core = g // 2, lax.rem(g, 2)
    levels = grps // 2
    twin = z * 2 + 1 - core

    loads = [
        pltpu.make_async_copy(px_hbm, px, in_sem.at[0]),
        pltpu.make_async_copy(pbc_hbm, pbc, in_sem.at[1]),
        pltpu.make_async_copy(rx_hbm, rx, in_sem.at[2]),
        pltpu.make_async_copy(rbc_hbm, rbc.at[pl.ds(2 * TILE, tiles * TILE)], in_sem.at[3]),
    ]
    for load in loads:
        load.start()

    barrier = pltpu.get_barrier_semaphore()
    for step in range(1, seqs):
        pl.semaphore_signal(barrier, inc=1, device_id={"seq": lax.rem(me + step, seqs)}, device_id_type=MESH)
    pl.semaphore_signal(barrier, inc=1, device_id={"grp": twin}, device_id_type=MESH)

    @pl.when(z > 0)
    def _():
        pl.semaphore_signal(barrier, inc=1, device_id={"grp": g - 2}, device_id_type=MESH)

    @pl.when(z < levels - 1)
    def _():
        pl.semaphore_signal(barrier, inc=1, device_id={"grp": g + 2}, device_id_type=MESH)

    pe[0] = spreader(TILE, cols, (32, 64))
    pe[1] = spreader(TILE, cols, (0, 32))
    re[0] = spreader(TILE, cb, (head_rows, 2 * head_rows))
    re[1] = spreader(TILE, cb, (3 * head_rows, 4 * head_rows))
    re[2] = spreader(TILE, cb, (5 * head_rows, 6 * head_rows))
    row8 = iota((8, heads), 0)
    skips = split(jnp.broadcast_to(d_ref[...], (8, heads)), 3)
    skip_rows = jnp.where(row8 == 0, skips[0], jnp.where(row8 == 1, skips[1], jnp.where(row8 == 2, skips[2], 0.0)))
    skip_wide = dot(skip_rows.astype(BF16), spreader(heads, cols, (0,)))
    dwide[...] = jnp.broadcast_to(jnp.sum(skip_wide, axis=0, keepdims=True), (8, cols))

    before = iota((TILE, TILE), 0) <= iota((TILE, TILE), 1)
    upper = jnp.where(before, 1.0, 0.0).astype(BF16)
    low_bias = jnp.where(iota((TILE, TILE), 1) <= iota((TILE, TILE), 0), 0.0, -1e30)

    prow = []
    for t in range(2):
        lanes = slice(t * TILE, (t + 1) * TILE)
        parts = split(pdec_ref[:, lanes], 3)
        sums = dot(jnp.concatenate(parts, axis=0).astype(BF16), upper)
        cum = sums[:heads] + sums[heads : 2 * heads] + sums[2 * heads :]
        dt = pdt_ref[:, lanes]
        c2 = cum * LOG2E
        prow.append(jnp.log2(dt) - c2)
        grown = split(jnp.exp2(c2), 2)
        weight = split(jnp.exp2(c2[:, TILE - 1 :] - c2) * dt, 2)
        fill = jnp.zeros((TILE - 3 * heads, TILE), F32)
        pt[2 * t] = jnp.concatenate([c2] + grown + [fill], axis=0).T
        fill = jnp.zeros((TILE - 2 * heads, TILE), F32)
        pt[2 * t + 1] = jnp.concatenate(weight + [fill], axis=0).T
    loads[0].wait()
    loads[1].wait()
    chunk = min(cols, 512)
    for t in range(2):
        rows = slice(t * TILE, (t + 1) * TILE)
        for start in range(0, cols, chunk):
            here = slice(start, start + chunk)
            wide = dot(pt[2 * t + 1].astype(BF16), pe[1, :, here])
            pv[t, :, here] = (px[rows, here].astype(F32) * wide).astype(BF16)
            last = dot(pt[2 * t, TILE - 8 :, :].astype(BF16), pe[0, :, here])
            ptot[t, :, here] = jnp.broadcast_to(last[7:8], (8, chunk))
    for s in range(seqs):
        here = slice(s * cb, (s + 1) * cb)
        t0, t1 = ptot[0, 0:1, here], ptot[1, 0:1, here]
        ended = t1 * dot_tn(pbc[0:TILE, :STATE], pv[0, :, here]) + dot_tn(pbc[TILE:, :STATE], pv[1, :, here])
        abuf[s, 0:STATE, :] = ended.astype(BF16)
        hi, lo = split(t0 * t1, 2)
        row = iota((16, cb), 0)
        abuf[s, STATE:, :] = jnp.where(row == 0, hi, jnp.where(row == 1, lo, 0.0)).astype(BF16)

    pl.semaphore_wait(barrier, seqs + jnp.where(z > 0, 1, 0) + jnp.where(z < levels - 1, 1, 0))

    def state_copy(step):
        peer = lax.rem(me + step, seqs)
        return pltpu.make_async_remote_copy(
            src_ref=abuf.at[peer], dst_ref=arecv.at[me], send_sem=a_send.at[step], recv_sem=a_recv.at[step],
            device_id={"seq": peer}, device_id_type=MESH)

    def prefix_copy(step):
        peer = lax.rem(me + step, seqs)
        return peer, pltpu.make_async_remote_copy(
            src_ref=pbuf.at[peer], dst_ref=precv.at[me], send_sem=x_send.at[step], recv_sem=x_recv.at[step],
            device_id={"seq": peer}, device_id_type=MESH)

    def seed_copy(level, target, send_sem):
        which = level * 2 + core
        return pltpu.make_async_remote_copy(
            src_ref=seeds.at[which], dst_ref=seeds.at[which], send_sem=send_sem, recv_sem=g_recv.at[which],
            device_id={"grp": target}, device_id_type=MESH)

    for step in range(1, seqs):
        state_copy(step).start()
    arecv[me] = abuf[me]

    for t in range(2):
        rows = slice(t * TILE, (t + 1) * TILE)
        b_rows, c_rows = pbc[rows, :STATE], pbc[rows, STATE:]
        scores = dot_nt(c_rows, b_rows)
        column = pt[2 * t]
        x_tile = px[rows, :]
        pieces = diagonal(column, prow[t], low_bias, scores, x_tile, heads)
        for pair, piece in enumerate(pieces):
            here = slice(pair * 2 * CHANNELS, (pair + 1) * 2 * CHANNELS)
            pacc[rows, here] = piece + dwide[0:1, here] * x_tile[:, here].astype(F32)
        if t == 1:
            cross = dot_nt(c_rows, pbc[0:TILE, :STATE]).astype(BF16)
            for start in range(0, cols, chunk):
                here = slice(start, start + chunk)
                grown = dot(column.astype(BF16), pe[0, :, here])
                pacc[rows, here] += grown * dot(cross, pv[0, :, here])

    limits, owners, edge = [], [], jnp.int32(0)
    for k in range(slots):
        which = pack_ref[0, k]
        there = which >= 0
        which = jnp.maximum(which, 0)
        owners.append(jnp.where(there, prm_ref[which], -1))
        limits.append(edge)
        edge = edge + jnp.where(there, len_ref[which], 0)
    limits.append(edge)

    rbc[0 : 2 * TILE, :] = jnp.zeros((2 * TILE, 2 * STATE), BF16)
    rv[0:2] = jnp.zeros((2, TILE, cb), BF16)
    rtot[0:2] = jnp.zeros((2, 8, cb), F32)
    parts = split(rdec_ref[...], 3)
    rdecs[:, 0 : 2 * TILE] = jnp.zeros((4 * head_rows, 2 * TILE), BF16)
    rdecs[:, 2 * TILE :] = jnp.concatenate(parts + [jnp.zeros_like(parts[0])], axis=0).astype(BF16)
    my_cols = pl.ds(pl.multiple_of(me * cb, cb), cb)
    loads[2].wait()
    loads[3].wait()

    def response_tile(tile, carry):
        base = pl.multiple_of(tile * TILE, TILE)
        rows = pl.ds(base, TILE)
        place = base + iota((8, TILE), 1)
        start = jnp.zeros((8, TILE), jnp.int32)
        owner = jnp.full((8, TILE), -1, jnp.int32)
        for k in range(slots):
            start = jnp.where(place >= limits[k], limits[k], start)
            owner = jnp.where((place >= limits[k]) & (place < limits[k + 1]), owners[k], owner)
        start = jnp.where(place >= limits[slots], limits[slots], start) - base

        j = iota((3 * TILE, TILE), 0) - 2 * TILE
        i = iota((3 * TILE, TILE), 1)
        ordered = j <= i
        in_slot = jnp.where(ordered & (j >= start[0:1]), 1.0, 0.0)
        in_tile = jnp.where(ordered & (j >= 0), 1.0, 0.0)
        sums = dot(rdecs[:, pl.ds(base, 3 * TILE)], jnp.concatenate([in_slot, in_tile], axis=1).astype(BF16))
        sums = sums[:head_rows] + sums[head_rows : 2 * head_rows] + sums[2 * head_rows : 3 * head_rows]
        gain, c2 = sums[:, :TILE] * LOG2E, sums[:, TILE:] * LOG2E
        dt = rdt_ref[:, rows]
        row_form = jnp.log2(dt) - c2
        where_rows = jnp.where(iota((8, TILE), 0) == 0, start, owner).astype(F32)
        stack = [c2] + split(jnp.exp2(c2), 2) + split(jnp.exp2(c2[:, TILE - 1 :] - c2) * dt, 2)
        stack += split(jnp.exp2(gain), 2) + [where_rows]
        stack += [jnp.zeros((TILE - 7 * head_rows - 8, TILE), F32)]
        column = jnp.concatenate(stack, axis=0).T
        rt[tile] = column
        narrow = column.astype(BF16)

        x_tile = rx[rows, :]
        wide = dot(narrow, re[1])
        rv[tile + 2] = (x_tile.astype(F32) * wide).astype(BF16)
        grown = dot(narrow, re[0])
        rtot[tile + 2] = jnp.broadcast_to(grown[TILE - 1 :], (8, cb))

        c_rows = rbc[pl.ds(base + 2 * TILE, TILE), STATE:]
        scores = dot_nt(c_rows, rbc[pl.ds(base, 3 * TILE), :STATE])
        j = iota((TILE, 3 * TILE), 1) - 2 * TILE
        first = column[:, 7 * head_rows : 7 * head_rows + 1].astype(jnp.int32)
        seen = (j <= iota((TILE, 3 * TILE), 0)) & (j >= first)
        bias = jnp.where(seen[:, 2 * TILE :], 0.0, -1e30)
        cross = jnp.where(seen[:, : 2 * TILE], scores[:, : 2 * TILE], 0.0).astype(BF16)
        earlier = dot(cross[:, TILE:], rv[tile + 1]) + rtot[tile + 1, 0:1] * dot(cross[:, :TILE], rv[tile])
        pieces = diagonal(column, row_form, bias, scores[:, 2 * TILE :], x_tile, block_heads)
        skip = dwide[0:1, my_cols]
        racc[rows, :] = jnp.concatenate(pieces, axis=1) + grown * earlier + skip * x_tile.astype(F32)
        return carry

    share = tiles // 4
    lax.fori_loop(0, share, response_tile, 0)

    for step in range(1, seqs):
        state_copy(step).wait_recv()
    ahead = jnp.zeros((STATE, cb), F32)
    for s in range(seqs):
        pbuf[s] = ahead.astype(BF16)
        decay = arecv[s, STATE:, :].astype(F32)
        ahead = (decay[0:1] + decay[1:2]) * ahead + arecv[s, 0:STATE, :].astype(F32)
    seeds[g] = ahead.astype(BF16)

    def pass_on(level, distance, up):
        if up:
            @pl.when(z < levels - 1)
            def _():
                seed_copy(level, g + 2, up_send.at[distance]).start()
        else:
            @pl.when(z > 0)
            def _():
                seed_copy(level, g - 2, down_send.at[distance]).start()

    pass_on(z, 0, True)
    pass_on(z, 0, False)
    seed_copy(z, twin, tu_send.at[0]).start()
    for step in range(1, seqs):
        peer, copy = prefix_copy(step)

        @pl.when(peer > 0)
        def _():
            copy.start()

    precv[me] = pbuf[me]

    def relay(distance):
        @pl.when(z >= distance)
        def _():
            seed_copy(z - distance, twin, tu_send.at[distance]).wait_recv()
            pass_on(z - distance, distance, True)
            seed_copy(z - distance, twin, tu_send.at[distance]).start()

        @pl.when(z + distance < levels)
        def _():
            seed_copy(z + distance, twin, td_send.at[distance]).wait_recv()
            pass_on(z + distance, distance, False)
            seed_copy(z + distance, twin, td_send.at[distance]).start()

    lax.fori_loop(share, 2 * share, response_tile, 0)
    relay(1)
    lax.fori_loop(2 * share, 3 * share, response_tile, 0)
    if levels > 2:
        relay(2)
    lax.fori_loop(3 * share, tiles, response_tile, 0)

    for step in range(1, seqs):
        copy = prefix_copy(step)[1]

        @pl.when(me > 0)
        def _():
            copy.wait_recv()

    @pl.when(me == 0)
    def _():
        for s in range(seqs):
            precv[s] = jnp.zeros((STATE, cb), BF16)

    p_outs = []
    for t in range(2):
        rows = slice(t * TILE, (t + 1) * TILE)
        narrow = pt[2 * t].astype(BF16)
        for s in range(seqs):
            here = slice(s * cb, (s + 1) * cb)
            grown = dot(narrow, pe[0, :, here])
            if t == 1:
                grown = grown * ptot[0, 0:1, here]
            carried = grown * dot(pbc[rows, STATE:], precv[s])
            pout[rows, here] = (pacc[rows, here] + carried).astype(BF16)
        p_outs.append(pltpu.make_async_copy(pout.at[rows], pout_hbm.at[rows], out_sem.at[tiles + t]))
        p_outs[-1].start()

    for distance in range(3, levels):
        relay(distance)
    for level in range(levels):
        which = level * 2 + 1 - core
        pltpu.make_async_remote_copy(
            src_ref=seeds.at[which], dst_ref=seeds.at[which], send_sem=tu_send.at[0], recv_sem=g_recv.at[which],
            device_id={"grp": twin}, device_id_type=MESH).wait_recv()

    def out_copy(tile):
        rows = pl.ds(pl.multiple_of(tile * TILE, TILE), TILE)
        return pltpu.make_async_copy(rout.at[rows], rout_hbm.at[rows], out_sem.at[tile])

    def seed_tile(tile, carry):
        base = pl.multiple_of(tile * TILE, TILE)
        rows = pl.ds(base, TILE)
        column = rt[tile]
        owner = column[:, 7 * head_rows + 1 : 7 * head_rows + 2].astype(jnp.int32)
        c_rows = rbc[pl.ds(base + 2 * TILE, TILE), STATE:].astype(F32)
        batch = 8 if grps % 8 == 0 else 2
        total = jnp.zeros((TILE, cb), F32)
        for q in range(0, grps, batch):
            chosen = [jnp.where(owner == q + n, c_rows, 0.0) for n in range(batch)]
            table = seeds[q : q + batch].reshape(batch * STATE, cb)
            total = total + dot(jnp.concatenate(chosen, axis=1).astype(BF16), table)
        result = racc[rows, :] + dot(column.astype(BF16), re[2]) * total
        rout[rows, :] = jnp.where(owner >= 0, result, 0.0).astype(BF16)
        out_copy(tile).start()
        return carry

    lax.fori_loop(0, tiles, seed_tile, 0)

    for step in range(1, seqs):
        state_copy(step).wait_send()
        peer, copy = prefix_copy(step)

        @pl.when(peer > 0)
        def _():
            copy.wait_send()

    for distance in range(levels):
        @pl.when((z >= distance) & (z < levels - 1))
        def _():
            seed_copy(z - distance, g + 2, up_send.at[distance]).wait_send()

        @pl.when((z + distance < levels) & (z > 0))
        def _():
            seed_copy(z + distance, g - 2, down_send.at[distance]).wait_send()

        @pl.when(z >= distance)
        def _():
            seed_copy(z - distance, twin, tu_send.at[distance]).wait_send()

        if distance > 0:
            @pl.when(z + distance < levels)
            def _():
                seed_copy(z + distance, twin, td_send.at[distance]).wait_send()

    for copy in p_outs:
        copy.wait()

    def out_wait(tile, carry):
        out_copy(tile).wait()
        return carry

    lax.fori_loop(0, tiles, out_wait, 0)


def on_device(
    p_x, p_bc, p_dt, p_decay, r_x, r_bc, r_dt, r_decay, pack_list, resp_len, resp_prompt, d_skip
):
    seqs, grps = lax.axis_size("seq"), lax.axis_size("grp")
    heads = p_dt.shape[1]
    block_heads = heads // seqs
    head_rows = max(8, block_heads)
    slots = pack_list.shape[1]
    tiles = r_x.shape[0] // TILE
    cols, cb = heads * CHANNELS, block_heads * CHANNELS
    if head_rows > block_heads:
        extra = ((0, head_rows - block_heads), (0, 0))
        r_dt, r_decay = jnp.pad(r_dt, extra, constant_values=1.0), jnp.pad(r_decay, extra)
    sizes = (seqs, grps, heads, block_heads, head_rows, slots, tiles)
    levels = grps // 2
    anywhere = pl.BlockSpec(memory_space=pl.ANY)
    vmem = pl.BlockSpec(memory_space=pltpu.VMEM)
    smem = pl.BlockSpec(memory_space=pltpu.SMEM)
    dma = pltpu.SemaphoreType.DMA
    p_out, r_out = pl.pallas_call(
        functools.partial(kernel, sizes),
        out_shape=(
            jax.ShapeDtypeStruct((2 * TILE, cols), BF16),
            jax.ShapeDtypeStruct((tiles * TILE, cb), BF16),
        ),
        in_specs=[anywhere, anywhere, vmem, vmem, anywhere, anywhere, vmem, vmem, smem, smem, smem, vmem],
        out_specs=(anywhere, anywhere),
        scratch_shapes=[
            pltpu.VMEM((2 * TILE, cols), BF16),
            pltpu.VMEM((2 * TILE, 2 * STATE), BF16),
            pltpu.VMEM((tiles * TILE, cb), BF16),
            pltpu.VMEM(((tiles + 2) * TILE, 2 * STATE), BF16),
            pltpu.VMEM((2, TILE, cols), BF16),
            pltpu.VMEM((4, TILE, TILE), F32),
            pltpu.VMEM((2, TILE, cols), BF16),
            pltpu.VMEM((2, 8, cols), F32),
            pltpu.VMEM((2 * TILE, cols), F32),
            pltpu.VMEM((8, cols), F32),
            pltpu.VMEM((tiles + 2, TILE, cb), BF16),
            pltpu.VMEM((tiles, TILE, TILE), F32),
            pltpu.VMEM((3, TILE, cb), BF16),
            pltpu.VMEM((tiles + 2, 8, cb), F32),
            pltpu.VMEM((tiles * TILE, cb), F32),
            pltpu.VMEM((4 * head_rows, (tiles + 2) * TILE), BF16),
            pltpu.VMEM((seqs, STATE + 16, cb), BF16),
            pltpu.VMEM((seqs, STATE + 16, cb), BF16),
            pltpu.VMEM((seqs, STATE, cb), BF16),
            pltpu.VMEM((seqs, STATE, cb), BF16),
            pltpu.VMEM((grps, STATE, cb), BF16),
            pltpu.VMEM((2 * TILE, cols), BF16),
            pltpu.VMEM((tiles * TILE, cb), BF16),
            dma((4,)),
            dma((tiles + 2,)),
            dma((seqs,)),
            dma((seqs,)),
            dma((seqs,)),
            dma((seqs,)),
            dma((grps,)),
            dma((levels,)),
            dma((levels,)),
            dma((levels,)),
            dma((levels,)),
        ],
        compiler_params=pltpu.CompilerParams(
            collective_id=0, has_side_effects=True, vmem_limit_bytes=48 * 2**20
        ),
        cost_estimate=pl.CostEstimate(flops=4 * 10**9, bytes_accessed=8 * 10**6, transcendentals=4 * 10**6),
        name="scan_and_seeds",
    )(
        p_x[0], p_bc[0], p_dt[0], p_decay[0], r_x, r_bc, r_dt, r_decay,
        pack_list, resp_len, resp_prompt, d_skip[None],
    )
    return p_out[None], r_out


def solution(mesh):
    placed = (
        P("grp", "seq", None),
        P("grp", "seq", None),
        P("grp", None, "seq"),
        P("grp", None, "seq"),
        P("grp", "seq"),
        P("grp", None),
        P("seq", "grp"),
        P("seq", "grp"),
        P("grp", None),
        P(),
        P(),
        P(),
    )
    return jax.shard_map(
        on_device,
        mesh=mesh,
        in_specs=placed,
        out_specs=(P("grp", "seq", None), P("grp", "seq")),
        check_vma=False,
    )
```

time: 292 us -> 50 us (0.17)
  the two profiles are of different devices: /device:TPU:0 before, /device:TPU:1 now
where the time goes in v1:
time: 50 us; the launch traced here: 49.6 us
  Pallas kernels  37.5 us (75%)
  local copies, waits for them, and re-layouts  11.4 us (23%)
  between operations  0.66 us (1%)
    pallas_call x1, Pallas kernels, on_device(): pl.pallas_call(functools.partial(kernel, sizes), out_shape=(jax.ShapeDtyp...  37.5 us
    unnamed x24, local copies, waits for them, and re-layouts  11.4 us

profile of v1, /device:TPU:1, one launch (start us, length us, event | category | flops | bytes accessed | tf_op | source)
XLA Modules:
  0.0 49.6 jit_solution(11349356511938210576)
XLA Ops:
  0.6 0.0 copy-start
  0.6 1.2 %copy-done = bf16[1,256,2048]{2,1,0:T(8,128)(2,1)S(1)} copy-done((bf16[1,256,2048]{2,1,0:T(8,128)(2,1)S(1)}, bf16[1,256,2048]{2,1,0:T(8,128)(2,1)}, u32[]{:S(2)}) %copy-start) | copy-done | bytes 1048600
  1.9 0.0 copy-start.1
  1.9 1.2 %copy-done.1 = bf16[2048,256]{1,0:T(8,128)(2,1)S(1)} copy-done((bf16[2048,256]{1,0:T(8,128)(2,1)S(1)}, bf16[2048,256]{1,0:T(8,128)(2,1)}, u32[]{:S(2)}) %copy-start.1) | copy-done | bytes 1048600
  3.1 0.0 copy-start.2
  3.1 0.9 %copy-done.2 = bf16[1,256,256]{2,1,0:T(8,128)(2,1)S(1)} copy-done((bf16[1,256,256]{2,1,0:T(8,128)(2,1)S(1)}, bf16[1,256,256]{2,1,0:T(8,128)(2,1)}, u32[]{:S(2)}) %copy-start.2) | copy-done | bytes 131096
  4.0 0.0 copy-start.3
  4.0 0.8 %copy-done.3 = f32[8,2048]{1,0:T(8,128)S(1)} copy-done((f32[8,2048]{1,0:T(8,128)S(1)}, f32[8,2048]{1,0:T(8,128)}, u32[]{:S(2)}) %copy-start.3) | copy-done | bytes 65560
  4.8 0.0 copy-start.4
  4.8 0.8 %copy-done.4 = f32[8,2048]{1,0:T(8,128)S(1)} copy-done((f32[8,2048]{1,0:T(8,128)S(1)}, f32[8,2048]{1,0:T(8,128)}, u32[]{:S(2)}) %copy-start.4) | copy-done | bytes 65560
  5.7 0.0 copy-start.5
  5.7 0.8 %copy-done.5 = f32[1,32,256]{2,1,0:T(8,128)S(1)} copy-done((f32[1,32,256]{2,1,0:T(8,128)S(1)}, f32[1,32,256]{2,1,0:T(8,128)}, u32[]{:S(2)}) %copy-start.5) | copy-done | bytes 32792
  6.4 0.0 copy-start.6
  6.4 0.8 %copy-done.6 = f32[1,32,256]{2,1,0:T(8,128)S(1)} copy-done((f32[1,32,256]{2,1,0:T(8,128)S(1)}, f32[1,32,256]{2,1,0:T(8,128)}, u32[]{:S(2)}) %copy-start.6) | copy-done | bytes 32792
  7.2 0.0 copy-start.7
  7.2 0.7 %copy-done.7 = s32[1,8]{1,0:T(1,128)S(1)} copy-done((s32[1,8]{1,0:T(1,128)S(1)}, s32[1,8]{1,0:T(1,128)}, u32[]{:S(2)}) %copy-start.7) | copy-done | bytes 56
  7.8 0.0 copy-start.8
  7.8 0.7 %copy-done.8 = s32[48]{0:T(128)S(1)} copy-done((s32[48]{0:T(128)S(1)}, s32[48]{0:T(128)}, u32[]{:S(2)}) %copy-start.8) | copy-done | bytes 216
  8.5 0.0 copy-start.9
  8.5 0.7 %copy-done.9 = s32[48]{0:T(128)S(1)} copy-done((s32[48]{0:T(128)S(1)}, s32[48]{0:T(128)}, u32[]{:S(2)}) %copy-start.9) | copy-done | bytes 216
  9.2 0.0 copy-start.10
  9.2 0.7 %copy-done.10 = f32[32]{0:T(128)S(1)} copy-done((f32[32]{0:T(128)S(1)}, f32[32]{0:T(128)}, u32[]{:S(2)}) %copy-start.10) | copy-done | bytes 152
  9.8 37.5 %scan_and_seeds.1 = (bf16[256,2048]{1,0:T(8,128)(2,1)S(1)}, bf16[2048,512]{1,0:T(8,128)(2,1)S(1)}) custom-call(bf16[256,2048]{1,0:T(8,128)(2,1)S(1)} %bitcast.7, bf16[256,256]{1,0:T(8,128)(2,1)S(1)} %bitcast.8, f32[32,256]{1,0:T(8,128)S(1)} %bitcast.9, f32[32,256]{1,0:T(8,128)S(1)} %bitcast.10, bf16[2048,512]{1,0:T(8,128)(2,1)} %rx_hbm.1, ...), custom_call_target="tpu_custom_call" | custom-call | flops 4000000000 | bytes 8000000 | tf_op jit(solution)/shard_map/scan_and_seeds/pallas_call | solution.py:435
  47.3 1.0 %copy.16 = bf16[1,256,2048]{2,1,0:T(8,128)(2,1)} copy(bf16[1,256,2048]{2,1,0:T(8,128)(2,1)S(1)} %bitcast.6) | data formatting | bytes 2097152
  48.2 1.3 %copy.17 = bf16[2048,512]{1,0:T(8,128)(2,1)} copy(bf16[2048,512]{1,0:T(8,128)(2,1)S(1)} %get-tuple-element.9) | data formatting | bytes 4194304
Async XLA Ops:
  0.6 1.2 %copy-start = (bf16[1,256,2048]{2,1,0:T(8,128)(2,1)S(1)}, bf16[1,256,2048]{2,1,0:T(8,128)(2,1)}, u32[]{:S(2)}) copy-start(bf16[1,256,2048]{2,1,0:T(8,128)(2,1)} %param.12) | copy-start | bytes 3145732
  1.9 1.2 %copy-start.1 = (bf16[2048,256]{1,0:T(8,128)(2,1)S(1)}, bf16[2048,256]{1,0:T(8,128)(2,1)}, u32[]{:S(2)}) copy-start(bf16[2048,256]{1,0:T(8,128)(2,1)} %rbc_hbm.1) | copy-start | bytes 3145732
  3.1 0.9 %copy-start.2 = (bf16[1,256,256]{2,1,0:T(8,128)(2,1)S(1)}, bf16[1,256,256]{2,1,0:T(8,128)(2,1)}, u32[]{:S(2)}) copy-start(bf16[1,256,256]{2,1,0:T(8,128)(2,1)} %param.13) | copy-start | bytes 393220
  4.0 0.8 %copy-start.3 = (f32[8,2048]{1,0:T(8,128)S(1)}, f32[8,2048]{1,0:T(8,128)}, u32[]{:S(2)}) copy-start(f32[8,2048]{1,0:T(8,128)} %rdt_ref.1) | copy-start | bytes 196612
  4.8 0.8 %copy-start.4 = (f32[8,2048]{1,0:T(8,128)S(1)}, f32[8,2048]{1,0:T(8,128)}, u32[]{:S(2)}) copy-start(f32[8,2048]{1,0:T(8,128)} %rdec_ref.1) | copy-start | bytes 196612
  5.7 0.8 %copy-start.5 = (f32[1,32,256]{2,1,0:T(8,128)S(1)}, f32[1,32,256]{2,1,0:T(8,128)}, u32[]{:S(2)}) copy-start(f32[1,32,256]{2,1,0:T(8,128)} %param.14) | copy-start | bytes 98308
  6.4 0.8 %copy-start.6 = (f32[1,32,256]{2,1,0:T(8,128)S(1)}, f32[1,32,256]{2,1,0:T(8,128)}, u32[]{:S(2)}) copy-start(f32[1,32,256]{2,1,0:T(8,128)} %param.15) | copy-start | bytes 98308
  7.2 0.7 %copy-start.7 = (s32[1,8]{1,0:T(1,128)S(1)}, s32[1,8]{1,0:T(1,128)}, u32[]{:S(2)}) copy-start(s32[1,8]{1,0:T(1,128)} %pack_ref.1) | copy-start | bytes 100
  7.8 0.7 %copy-start.8 = (s32[48]{0:T(128)S(1)}, s32[48]{0:T(128)}, u32[]{:S(2)}) copy-start(s32[48]{0:T(128)} %len_ref.1) | copy-start | bytes 580
  8.5 0.7 %copy-start.9 = (s32[48]{0:T(128)S(1)}, s32[48]{0:T(128)}, u32[]{:S(2)}) copy-start(s32[48]{0:T(128)} %prm_ref.1) | copy-start | bytes 580
  9.2 0.7 %copy-start.10 = (f32[32]{0:T(128)S(1)}, f32[32]{0:T(128)}, u32[]{:S(2)}) copy-start(f32[32]{0:T(128)} %param.23) | copy-start | bytes 388

commit v2 on v1

--- a/solution.py
+++ b/solution.py
@@ -70,8 +70,9 @@
 
 def kernel(
     sizes,
-    px_hbm, pbc_hbm, pdt_ref, pdec_ref, rx_hbm, rbc_hbm, rdt_ref, rdec_ref, pack_ref, len_ref, prm_ref, d_ref,
+    px_hbm, pbc_hbm, pdt_hbm, pdec_hbm, rx_hbm, rbc_hbm, rdt_hbm, rdec_hbm, pack_hbm, len_hbm, prm_hbm, d_hbm,
     pout_hbm, rout_hbm,
+    pdt_ref, pdec_ref, rdt, rdec_ref, pack_ref, len_ref, prm_ref, d_ref, rrow,
     px, pbc, rx, rbc, pv, pt, pe, ptot, pacc, dwide, rv, rt, re, rtot, racc, rdecs,
     abuf, arecv, pbuf, precv, seeds, pout, rout,
     in_sem, out_sem, a_send, a_recv, x_send, x_recv, g_recv, up_send, down_send, tu_send, td_send,
@@ -91,8 +92,11 @@
         pltpu.make_async_copy(rx_hbm, rx, in_sem.at[2]),
         pltpu.make_async_copy(rbc_hbm, rbc.at[pl.ds(2 * TILE, tiles * TILE)], in_sem.at[3]),
     ]
-    for load in loads:
-        load.start()
+    small = [(pdec_hbm, pdec_ref), (pdt_hbm, pdt_ref), (d_hbm, d_ref), (pack_hbm, pack_ref), (len_hbm, len_ref),
+             (prm_hbm, prm_ref), (rdec_hbm, rdec_ref), (rdt_hbm, rdt)]
+    loads += [pltpu.make_async_copy(src, dst, in_sem.at[4 + n]) for n, (src, dst) in enumerate(small)]
+    for n in (4, 5, 0, 1, 6, 7, 8, 9, 10, 11, 2, 3):
+        loads[n].start()
 
     barrier = pltpu.get_barrier_semaphore()
     for step in range(1, seqs):
@@ -112,6 +116,8 @@
     re[0] = spreader(TILE, cb, (head_rows, 2 * head_rows))
     re[1] = spreader(TILE, cb, (3 * head_rows, 4 * head_rows))
     re[2] = spreader(TILE, cb, (5 * head_rows, 6 * head_rows))
+    for n in (4, 5, 6):
+        loads[n].wait()
     row8 = iota((8, heads), 0)
     skips = split(jnp.broadcast_to(d_ref[...], (8, heads)), 3)
     skip_rows = jnp.where(row8 == 0, skips[0], jnp.where(row8 == 1, skips[1], jnp.where(row8 == 2, skips[2], 0.0)))
@@ -198,6 +204,8 @@
                 grown = dot(column.astype(BF16), pe[0, :, here])
                 pacc[rows, here] += grown * dot(cross, pv[0, :, here])
 
+    for n in range(7, 12):
+        loads[n].wait()
     limits, owners, edge = [], [], jnp.int32(0)
     for k in range(slots):
         which = pack_ref[0, k]
@@ -218,7 +226,7 @@
     loads[2].wait()
     loads[3].wait()
 
-    def response_tile(tile, carry):
+    def prepare(tile):
         base = pl.multiple_of(tile * TILE, TILE)
         rows = pl.ds(base, TILE)
         place = base + iota((8, TILE), 1)
@@ -237,22 +245,33 @@
         sums = dot(rdecs[:, pl.ds(base, 3 * TILE)], jnp.concatenate([in_slot, in_tile], axis=1).astype(BF16))
         sums = sums[:head_rows] + sums[head_rows : 2 * head_rows] + sums[2 * head_rows : 3 * head_rows]
         gain, c2 = sums[:, :TILE] * LOG2E, sums[:, TILE:] * LOG2E
-        dt = rdt_ref[:, rows]
-        row_form = jnp.log2(dt) - c2
+        dt = rdt[:, rows]
         where_rows = jnp.where(iota((8, TILE), 0) == 0, start, owner).astype(F32)
         stack = [c2] + split(jnp.exp2(c2), 2) + split(jnp.exp2(c2[:, TILE - 1 :] - c2) * dt, 2)
         stack += split(jnp.exp2(gain), 2) + [where_rows]
         stack += [jnp.zeros((TILE - 7 * head_rows - 8, TILE), F32)]
         column = jnp.concatenate(stack, axis=0).T
-        rt[tile] = column
-        narrow = column.astype(BF16)
-
+        wide = dot(column.astype(BF16), re[1])
+        last = dot(column[TILE - 8 :].astype(BF16), re[0])
+        scaled = (rx[rows, :].astype(F32) * wide).astype(BF16)
+        return column, jnp.log2(dt) - c2, scaled, jnp.broadcast_to(last[7:8], (8, cb))
+
+    def prepare_some(step, carry):
+        places = [step * together + n for n in range(together)]
+        made = [prepare(tile) for tile in places]
+        for tile, (column, row_form, scaled, last) in zip(places, made):
+            rt[tile] = column
+            rrow[tile] = row_form
+            rv[tile + 2] = scaled
+            rtot[tile + 2] = last
+        return carry
+
+    def within(tile):
+        base = pl.multiple_of(tile * TILE, TILE)
+        rows = pl.ds(base, TILE)
+        column = rt[tile]
         x_tile = rx[rows, :]
-        wide = dot(narrow, re[1])
-        rv[tile + 2] = (x_tile.astype(F32) * wide).astype(BF16)
-        grown = dot(narrow, re[0])
-        rtot[tile + 2] = jnp.broadcast_to(grown[TILE - 1 :], (8, cb))
-
+        grown = dot(column.astype(BF16), re[0])
         c_rows = rbc[pl.ds(base + 2 * TILE, TILE), STATE:]
         scores = dot_nt(c_rows, rbc[pl.ds(base, 3 * TILE), :STATE])
         j = iota((TILE, 3 * TILE), 1) - 2 * TILE
@@ -261,13 +280,22 @@
         bias = jnp.where(seen[:, 2 * TILE :], 0.0, -1e30)
         cross = jnp.where(seen[:, : 2 * TILE], scores[:, : 2 * TILE], 0.0).astype(BF16)
         earlier = dot(cross[:, TILE:], rv[tile + 1]) + rtot[tile + 1, 0:1] * dot(cross[:, :TILE], rv[tile])
-        pieces = diagonal(column, row_form, bias, scores[:, 2 * TILE :], x_tile, block_heads)
+        pieces = diagonal(column, rrow[tile], bias, scores[:, 2 * TILE :], x_tile, block_heads)
         skip = dwide[0:1, my_cols]
-        racc[rows, :] = jnp.concatenate(pieces, axis=1) + grown * earlier + skip * x_tile.astype(F32)
+        return jnp.concatenate(pieces, axis=1) + grown * earlier + skip * x_tile.astype(F32)
+
+    def response_tiles(step, carry):
+        places = [step * 2 + n for n in range(2)]
+        made = [within(tile) for tile in places]
+        for tile, total in zip(places, made):
+            racc[pl.ds(pl.multiple_of(tile * TILE, TILE), TILE), :] = total
         return carry
 
-    share = tiles // 4
-    lax.fori_loop(0, share, response_tile, 0)
+    together = 4
+    lax.fori_loop(0, tiles // together, prepare_some, 0)
+
+    share = tiles // 8
+    lax.fori_loop(0, share, response_tiles, 0)
 
     for step in range(1, seqs):
         state_copy(step).wait_recv()
@@ -313,12 +341,12 @@
             pass_on(z + distance, distance, False)
             seed_copy(z + distance, twin, td_send.at[distance]).start()
 
-    lax.fori_loop(share, 2 * share, response_tile, 0)
+    lax.fori_loop(share, 2 * share, response_tiles, 0)
     relay(1)
-    lax.fori_loop(2 * share, 3 * share, response_tile, 0)
+    lax.fori_loop(2 * share, 3 * share, response_tiles, 0)
     if levels > 2:
         relay(2)
-    lax.fori_loop(3 * share, tiles, response_tile, 0)
+    lax.fori_loop(3 * share, 4 * share, response_tiles, 0)
 
     for step in range(1, seqs):
         copy = prefix_copy(step)[1]
@@ -358,9 +386,8 @@
         rows = pl.ds(pl.multiple_of(tile * TILE, TILE), TILE)
         return pltpu.make_async_copy(rout.at[rows], rout_hbm.at[rows], out_sem.at[tile])
 
-    def seed_tile(tile, carry):
+    def seeded(tile):
         base = pl.multiple_of(tile * TILE, TILE)
-        rows = pl.ds(base, TILE)
         column = rt[tile]
         owner = column[:, 7 * head_rows + 1 : 7 * head_rows + 2].astype(jnp.int32)
         c_rows = rbc[pl.ds(base + 2 * TILE, TILE), STATE:].astype(F32)
@@ -370,12 +397,18 @@
             chosen = [jnp.where(owner == q + n, c_rows, 0.0) for n in range(batch)]
             table = seeds[q : q + batch].reshape(batch * STATE, cb)
             total = total + dot(jnp.concatenate(chosen, axis=1).astype(BF16), table)
-        result = racc[rows, :] + dot(column.astype(BF16), re[2]) * total
-        rout[rows, :] = jnp.where(owner >= 0, result, 0.0).astype(BF16)
-        out_copy(tile).start()
+        result = racc[pl.ds(base, TILE), :] + dot(column.astype(BF16), re[2]) * total
+        return jnp.where(owner >= 0, result, 0.0).astype(BF16)
+
+    def seed_tiles(step, carry):
+        places = [step * 2 + n for n in range(2)]
+        made = [seeded(tile) for tile in places]
+        for tile, result in zip(places, made):
+            rout[pl.ds(pl.multiple_of(tile * TILE, TILE), TILE), :] = result
+            out_copy(tile).start()
         return carry
 
-    lax.fori_loop(0, tiles, seed_tile, 0)
+    lax.fori_loop(0, tiles // 2, seed_tiles, 0)
 
     for step in range(1, seqs):
         state_copy(step).wait_send()
@@ -429,8 +462,6 @@
     sizes = (seqs, grps, heads, block_heads, head_rows, slots, tiles)
     levels = grps // 2
     anywhere = pl.BlockSpec(memory_space=pl.ANY)
-    vmem = pl.BlockSpec(memory_space=pltpu.VMEM)
-    smem = pl.BlockSpec(memory_space=pltpu.SMEM)
     dma = pltpu.SemaphoreType.DMA
     p_out, r_out = pl.pallas_call(
         functools.partial(kernel, sizes),
@@ -438,9 +469,18 @@
             jax.ShapeDtypeStruct((2 * TILE, cols), BF16),
             jax.ShapeDtypeStruct((tiles * TILE, cb), BF16),
         ),
-        in_specs=[anywhere, anywhere, vmem, vmem, anywhere, anywhere, vmem, vmem, smem, smem, smem, vmem],
+        in_specs=[pl.BlockSpec(memory_space=pltpu.HBM)] * 12,
         out_specs=(anywhere, anywhere),
         scratch_shapes=[
+            pltpu.VMEM(p_dt.shape[1:], F32),
+            pltpu.VMEM(p_decay.shape[1:], F32),
+            pltpu.VMEM(r_dt.shape, F32),
+            pltpu.VMEM(r_decay.shape, F32),
+            pltpu.SMEM(pack_list.shape, jnp.int32),
+            pltpu.SMEM(resp_len.shape, jnp.int32),
+            pltpu.SMEM(resp_prompt.shape, jnp.int32),
+            pltpu.VMEM((1, heads), F32),
+            pltpu.VMEM((tiles, head_rows, TILE), F32),
             pltpu.VMEM((2 * TILE, cols), BF16),
             pltpu.VMEM((2 * TILE, 2 * STATE), BF16),
             pltpu.VMEM((tiles * TILE, cb), BF16),
@@ -464,7 +504,7 @@
             pltpu.VMEM((grps, STATE, cb), BF16),
             pltpu.VMEM((2 * TILE, cols), BF16),
             pltpu.VMEM((tiles * TILE, cb), BF16),
-            dma((4,)),
+            dma((12,)),
             dma((tiles + 2,)),
             dma((seqs,)),
             dma((seqs,)),

time: 50 us -> 49.6 us (level)
  Pallas kernels: 37.5 us -> 37 us
where the time goes in v2:
time: 49.6 us; the launch traced here: 49.1 us
  Pallas kernels  37 us (75%)
  local copies, waits for them, and re-layouts  11.4 us (23%)
  between operations  0.66 us (1%)
    pallas_call x1, Pallas kernels, on_device(): pl.pallas_call(functools.partial(kernel, sizes), out_shape=(jax.ShapeDtyp...  37 us
    unnamed x24, local copies, waits for them, and re-layouts  11.4 us

profile of v2, /device:TPU:1, one launch (start us, length us, event | category | flops | bytes accessed | tf_op | source)
XLA Modules:
  0.0 49.1 jit_solution(7689415302460375055)
XLA Ops:
  0.6 0.0 copy-start
  0.6 1.2 %copy-done = bf16[1,256,2048]{2,1,0:T(8,128)(2,1)S(1)} copy-done((bf16[1,256,2048]{2,1,0:T(8,128)(2,1)S(1)}, bf16[1,256,2048]{2,1,0:T(8,128)(2,1)}, u32[]{:S(2)}) %copy-start) | copy-done | bytes 1048600
  1.9 0.0 copy-start.1
  1.9 1.2 %copy-done.1 = bf16[2048,256]{1,0:T(8,128)(2,1)S(1)} copy-done((bf16[2048,256]{1,0:T(8,128)(2,1)S(1)}, bf16[2048,256]{1,0:T(8,128)(2,1)}, u32[]{:S(2)}) %copy-start.1) | copy-done | bytes 1048600
  3.1 0.0 copy-start.2
  3.1 0.9 %copy-done.2 = bf16[1,256,256]{2,1,0:T(8,128)(2,1)S(1)} copy-done((bf16[1,256,256]{2,1,0:T(8,128)(2,1)S(1)}, bf16[1,256,256]{2,1,0:T(8,128)(2,1)}, u32[]{:S(2)}) %copy-start.2) | copy-done | bytes 131096
  4.0 0.0 copy-start.3
  4.0 0.8 %copy-done.3 = f32[8,2048]{1,0:T(8,128)S(1)} copy-done((f32[8,2048]{1,0:T(8,128)S(1)}, f32[8,2048]{1,0:T(8,128)}, u32[]{:S(2)}) %copy-start.3) | copy-done | bytes 65560
  4.8 0.0 copy-start.4
  4.8 0.8 %copy-done.4 = f32[8,2048]{1,0:T(8,128)S(1)} copy-done((f32[8,2048]{1,0:T(8,128)S(1)}, f32[8,2048]{1,0:T(8,128)}, u32[]{:S(2)}) %copy-start.4) | copy-done | bytes 65560
  5.7 0.0 copy-start.5
  5.7 0.8 %copy-done.5 = f32[1,32,256]{2,1,0:T(8,128)S(1)} copy-done((f32[1,32,256]{2,1,0:T(8,128)S(1)}, f32[1,32,256]{2,1,0:T(8,128)}, u32[]{:S(2)}) %copy-start.5) | copy-done | bytes 32792
  6.4 0.0 copy-start.6
  6.4 0.8 %copy-done.6 = f32[1,32,256]{2,1,0:T(8,128)S(1)} copy-done((f32[1,32,256]{2,1,0:T(8,128)S(1)}, f32[1,32,256]{2,1,0:T(8,128)}, u32[]{:S(2)}) %copy-start.6) | copy-done | bytes 32792
  7.2 0.0 copy-start.7
  7.2 0.7 %copy-done.7 = s32[1,8]{1,0:T(1,128)S(1)} copy-done((s32[1,8]{1,0:T(1,128)S(1)}, s32[1,8]{1,0:T(1,128)}, u32[]{:S(2)}) %copy-start.7) | copy-done | bytes 56
  7.8 0.0 copy-start.8
  7.8 0.7 %copy-done.8 = s32[48]{0:T(128)S(1)} copy-done((s32[48]{0:T(128)S(1)}, s32[48]{0:T(128)}, u32[]{:S(2)}) %copy-start.8) | copy-done | bytes 216
  8.5 0.0 copy-start.9
  8.5 0.7 %copy-done.9 = s32[48]{0:T(128)S(1)} copy-done((s32[48]{0:T(128)S(1)}, s32[48]{0:T(128)}, u32[]{:S(2)}) %copy-start.9) | copy-done | bytes 216
  9.2 0.0 copy-start.10
  9.2 0.7 %copy-done.10 = f32[32]{0:T(128)S(1)} copy-done((f32[32]{0:T(128)S(1)}, f32[32]{0:T(128)}, u32[]{:S(2)}) %copy-start.10) | copy-done | bytes 152
  9.8 37.0 %scan_and_seeds.1 = (bf16[256,2048]{1,0:T(8,128)(2,1)S(1)}, bf16[2048,512]{1,0:T(8,128)(2,1)S(1)}) custom-call(bf16[256,2048]{1,0:T(8,128)(2,1)S(1)} %bitcast.7, bf16[256,256]{1,0:T(8,128)(2,1)S(1)} %bitcast.8, f32[32,256]{1,0:T(8,128)S(1)} %bitcast.9, f32[32,256]{1,0:T(8,128)S(1)} %bitcast.10, bf16[2048,512]{1,0:T(8,128)(2,1)} %rx_hbm.1, ...), custom_call_target="tpu_custom_call" | custom-call | flops 4000000000 | bytes 8000000 | tf_op jit(solution)/shard_map/scan_and_seeds/pallas_call | solution.py:466
  46.8 1.0 %copy.16 = bf16[1,256,2048]{2,1,0:T(8,128)(2,1)} copy(bf16[1,256,2048]{2,1,0:T(8,128)(2,1)S(1)} %bitcast.6) | data formatting | bytes 2097152
  47.8 1.3 %copy.17 = bf16[2048,512]{1,0:T(8,128)(2,1)} copy(bf16[2048,512]{1,0:T(8,128)(2,1)S(1)} %get-tuple-element.9) | data formatting | bytes 4194304
Async XLA Ops:
  0.6 1.2 %copy-start = (bf16[1,256,2048]{2,1,0:T(8,128)(2,1)S(1)}, bf16[1,256,2048]{2,1,0:T(8,128)(2,1)}, u32[]{:S(2)}) copy-start(bf16[1,256,2048]{2,1,0:T(8,128)(2,1)} %param.12) | copy-start | bytes 3145732
  1.9 1.2 %copy-start.1 = (bf16[2048,256]{1,0:T(8,128)(2,1)S(1)}, bf16[2048,256]{1,0:T(8,128)(2,1)}, u32[]{:S(2)}) copy-start(bf16[2048,256]{1,0:T(8,128)(2,1)} %rbc_hbm.1) | copy-start | bytes 3145732
  3.1 0.9 %copy-start.2 = (bf16[1,256,256]{2,1,0:T(8,128)(2,1)S(1)}, bf16[1,256,256]{2,1,0:T(8,128)(2,1)}, u32[]{:S(2)}) copy-start(bf16[1,256,256]{2,1,0:T(8,128)(2,1)} %param.13) | copy-start | bytes 393220
  4.0 0.8 %copy-start.3 = (f32[8,2048]{1,0:T(8,128)S(1)}, f32[8,2048]{1,0:T(8,128)}, u32[]{:S(2)}) copy-start(f32[8,2048]{1,0:T(8,128)} %rdt_hbm.1) | copy-start | bytes 196612
  4.8 0.8 %copy-start.4 = (f32[8,2048]{1,0:T(8,128)S(1)}, f32[8,2048]{1,0:T(8,128)}, u32[]{:S(2)}) copy-start(f32[8,2048]{1,0:T(8,128)} %rdec_hbm.1) | copy-start | bytes 196612
  5.7 0.8 %copy-start.5 = (f32[1,32,256]{2,1,0:T(8,128)S(1)}, f32[1,32,256]{2,1,0:T(8,128)}, u32[]{:S(2)}) copy-start(f32[1,32,256]{2,1,0:T(8,128)} %param.14) | copy-start | bytes 98308
  6.4 0.8 %copy-start.6 = (f32[1,32,256]{2,1,0:T(8,128)S(1)}, f32[1,32,256]{2,1,0:T(8,128)}, u32[]{:S(2)}) copy-start(f32[1,32,256]{2,1,0:T(8,128)} %param.15) | copy-start | bytes 98308
  7.2 0.7 %copy-start.7 = (s32[1,8]{1,0:T(1,128)S(1)}, s32[1,8]{1,0:T(1,128)}, u32[]{:S(2)}) copy-start(s32[1,8]{1,0:T(1,128)} %pack_hbm.1) | copy-start | bytes 100
  7.8 0.7 %copy-start.8 = (s32[48]{0:T(128)S(1)}, s32[48]{0:T(128)}, u32[]{:S(2)}) copy-start(s32[48]{0:T(128)} %len_hbm.1) | copy-start | bytes 580
  8.5 0.7 %copy-start.9 = (s32[48]{0:T(128)S(1)}, s32[48]{0:T(128)}, u32[]{:S(2)}) copy-start(s32[48]{0:T(128)} %prm_hbm.1) | copy-start | bytes 580
  9.2 0.7 %copy-start.10 = (f32[32]{0:T(128)S(1)}, f32[32]{0:T(128)}, u32[]{:S(2)}) copy-start(f32[32]{0:T(128)} %param.23) | copy-start | bytes 388

commit v3 on v2

--- a/solution.py
+++ b/solution.py
@@ -204,6 +204,37 @@
                 grown = dot(column.astype(BF16), pe[0, :, here])
                 pacc[rows, here] += grown * dot(cross, pv[0, :, here])
 
+    for step in range(1, seqs):
+        state_copy(step).wait_recv()
+    ahead = jnp.zeros((STATE, cb), F32)
+    for s in range(seqs):
+        pbuf[s] = ahead.astype(BF16)
+        decay = arecv[s, STATE:, :].astype(F32)
+        ahead = (decay[0:1] + decay[1:2]) * ahead + arecv[s, 0:STATE, :].astype(F32)
+    seeds[g] = ahead.astype(BF16)
+
+    def pass_on(level, distance, up):
+        if up:
+            @pl.when(z < levels - 1)
+            def _():
+                seed_copy(level, g + 2, up_send.at[distance]).start()
+        else:
+            @pl.when(z > 0)
+            def _():
+                seed_copy(level, g - 2, down_send.at[distance]).start()
+
+    pass_on(z, 0, True)
+    pass_on(z, 0, False)
+    seed_copy(z, twin, tu_send.at[0]).start()
+    for step in range(1, seqs):
+        peer, copy = prefix_copy(step)
+
+        @pl.when(peer > 0)
+        def _():
+            copy.start()
+
+    precv[me] = pbuf[me]
+
     for n in range(7, 12):
         loads[n].wait()
     limits, owners, edge = [], [], jnp.int32(0)
@@ -291,43 +322,6 @@
             racc[pl.ds(pl.multiple_of(tile * TILE, TILE), TILE), :] = total
         return carry
 
-    together = 4
-    lax.fori_loop(0, tiles // together, prepare_some, 0)
-
-    share = tiles // 8
-    lax.fori_loop(0, share, response_tiles, 0)
-
-    for step in range(1, seqs):
-        state_copy(step).wait_recv()
-    ahead = jnp.zeros((STATE, cb), F32)
-    for s in range(seqs):
-        pbuf[s] = ahead.astype(BF16)
-        decay = arecv[s, STATE:, :].astype(F32)
-        ahead = (decay[0:1] + decay[1:2]) * ahead + arecv[s, 0:STATE, :].astype(F32)
-    seeds[g] = ahead.astype(BF16)
-
-    def pass_on(level, distance, up):
-        if up:
-            @pl.when(z < levels - 1)
-            def _():
-                seed_copy(level, g + 2, up_send.at[distance]).start()
-        else:
-            @pl.when(z > 0)
-            def _():
-                seed_copy(level, g - 2, down_send.at[distance]).start()
-
-    pass_on(z, 0, True)
-    pass_on(z, 0, False)
-    seed_copy(z, twin, tu_send.at[0]).start()
-    for step in range(1, seqs):
-        peer, copy = prefix_copy(step)
-
-        @pl.when(peer > 0)
-        def _():
-            copy.start()
-
-    precv[me] = pbuf[me]
-
     def relay(distance):
         @pl.when(z >= distance)
         def _():
@@ -341,12 +335,16 @@
             pass_on(z + distance, distance, False)
             seed_copy(z + distance, twin, td_send.at[distance]).start()
 
-    lax.fori_loop(share, 2 * share, response_tiles, 0)
+    together = 4
+    share = tiles // 8
+    lax.fori_loop(0, tiles // together, prepare_some, 0)
     relay(1)
-    lax.fori_loop(2 * share, 3 * share, response_tiles, 0)
-    if levels > 2:
-        relay(2)
-    lax.fori_loop(3 * share, 4 * share, response_tiles, 0)
+    lax.fori_loop(0, share, response_tiles, 0)
+    for distance in range(2, levels):
+        relay(distance)
+        if distance < 4:
+            lax.fori_loop((distance - 1) * share, distance * share, response_tiles, 0)
+    lax.fori_loop((min(levels, 4) - 1) * share, 4 * share, response_tiles, 0)
 
     for step in range(1, seqs):
         copy = prefix_copy(step)[1]
@@ -374,8 +372,6 @@
         p_outs.append(pltpu.make_async_copy(pout.at[rows], pout_hbm.at[rows], out_sem.at[tiles + t]))
         p_outs[-1].start()
 
-    for distance in range(3, levels):
-        relay(distance)
     for level in range(levels):
         which = level * 2 + 1 - core
         pltpu.make_async_remote_copy(
@@ -517,7 +513,7 @@
             dma((levels,)),
         ],
         compiler_params=pltpu.CompilerParams(
-            collective_id=0, has_side_effects=True, vmem_limit_bytes=48 * 2**20
+            collective_id=0, has_side_effects=True, vmem_limit_bytes=63 * 2**20
         ),
         cost_estimate=pl.CostEstimate(flops=4 * 10**9, bytes_accessed=8 * 10**6, transcendentals=4 * 10**6),
         name="scan_and_seeds",

time: 49.6 us -> 42.1 us (0.85)
  the two profiles are of different devices: /device:TPU:1 before, /device:TPU:0 now
where the time goes in v3:
time: 42.1 us; the launch traced here: 42 us
  Pallas kernels  37.5 us (89%)
  local copies, waits for them, and re-layouts  3.78 us (9%)
  between operations  0.65 us (2%)
    pallas_call x1, Pallas kernels, on_device(): pl.pallas_call(functools.partial(kernel, sizes), out_shape=(jax.ShapeDtyp...  37.5 us
    unnamed x4, local copies, waits for them, and re-layouts  3.78 us

profile of v3, /device:TPU:0, one launch (start us, length us, event | category | flops | bytes accessed | tf_op | source)
XLA Modules:
  0.0 42.0 jit_solution(4731431575942439551)
XLA Ops:
  0.6 37.5 %scan_and_seeds.1 = (bf16[256,2048]{1,0:T(8,128)(2,1)}, bf16[2048,512]{1,0:T(8,128)(2,1)}) custom-call(bf16[256,2048]{1,0:T(8,128)(2,1)} %bitcast.7, bf16[256,256]{1,0:T(8,128)(2,1)} %bitcast.8, f32[32,256]{1,0:T(8,128)} %bitcast.9, f32[32,256]{1,0:T(8,128)} %bitcast.10, bf16[2048,512]{1,0:T(8,128)(2,1)} %rx_hbm.1, bf16[2048,256]{1,0:T(8,128)(2,1)} %rbc_hbm.1, ...), custom_call_target="tpu_custom_call" | custom-call | flops 4000000000 | bytes 8000000 | tf_op jit(solution)/shard_map/scan_and_seeds/pallas_call | solution.py:462
  38.2 0.0 copy-start
  38.2 2.5 %copy.16 = bf16[1,256,2048]{2,1,0:T(8,128)(2,1)} copy(bf16[1,256,2048]{2,1,0:T(8,128)(2,1)} %bitcast.6) | data formatting | bytes 2097152
  40.6 0.0 copy-done
  40.6 1.3 %copy.17 = bf16[2048,512]{1,0:T(8,128)(2,1)} copy(bf16[2048,512]{1,0:T(8,128)(2,1)S(1)} %copy-done) | data formatting | bytes 4194304
Async XLA Ops:
  38.2 2.5 %copy-start = (bf16[2048,512]{1,0:T(8,128)(2,1)S(1)}, bf16[2048,512]{1,0:T(8,128)(2,1)}, u32[]{:S(2)}) copy-start(bf16[2048,512]{1,0:T(8,128)(2,1)} %get-tuple-element.9) | copy-start | bytes 6291460

commit v4 on v3

--- a/solution.py
+++ b/solution.py
@@ -51,9 +51,9 @@
 
 
 def paired(x_pair):
-    first = iota(x_pair.shape, 1) < CHANNELS
-    wide = x_pair.astype(F32)
-    return jnp.concatenate([jnp.where(first, wide, 0.0), jnp.where(first, 0.0, wide)], axis=0).astype(BF16)
+    first = jnp.where(iota(x_pair.shape, 1) < CHANNELS, 1.0, 0.0).astype(BF16)
+    second = jnp.where(iota(x_pair.shape, 1) < CHANNELS, 0.0, 1.0).astype(BF16)
+    return jnp.concatenate([x_pair * first, x_pair * second], axis=0)
 
 
 def diagonal(column, row, bias, scores, x_tile, heads):
@@ -111,8 +111,10 @@
     def _():
         pl.semaphore_signal(barrier, inc=1, device_id={"grp": g + 2}, device_id_type=MESH)
 
-    pe[0] = spreader(TILE, cols, (32, 64))
-    pe[1] = spreader(TILE, cols, (0, 32))
+    each = spreader(heads, cols, (0,))
+    none = jnp.zeros((heads, cols), BF16)
+    pe[0] = jnp.concatenate([none, each, each, none], axis=0)
+    pe[1] = jnp.concatenate([each, each, none, none], axis=0)
     re[0] = spreader(TILE, cb, (head_rows, 2 * head_rows))
     re[1] = spreader(TILE, cb, (3 * head_rows, 4 * head_rows))
     re[2] = spreader(TILE, cb, (5 * head_rows, 6 * head_rows))
@@ -121,7 +123,7 @@
     row8 = iota((8, heads), 0)
     skips = split(jnp.broadcast_to(d_ref[...], (8, heads)), 3)
     skip_rows = jnp.where(row8 == 0, skips[0], jnp.where(row8 == 1, skips[1], jnp.where(row8 == 2, skips[2], 0.0)))
-    skip_wide = dot(skip_rows.astype(BF16), spreader(heads, cols, (0,)))
+    skip_wide = dot(skip_rows.astype(BF16), each)
     dwide[...] = jnp.broadcast_to(jnp.sum(skip_wide, axis=0, keepdims=True), (8, cols))
 
     before = iota((TILE, TILE), 0) <= iota((TILE, TILE), 1)

time: 42.1 us -> 42.2 us (level)
  no operation moved by 1% of the time
where the time goes in v4:
time: 42.2 us; the launch traced here: 42 us
  Pallas kernels  37.6 us (89%)
  local copies, waits for them, and re-layouts  3.78 us (9%)
  between operations  0.65 us (2%)
    pallas_call x1, Pallas kernels, on_device(): pl.pallas_call(functools.partial(kernel, sizes), out_shape=(jax.ShapeDtyp...  37.6 us
    unnamed x4, local copies, waits for them, and re-layouts  3.78 us

profile of v4, /device:TPU:0, one launch (start us, length us, event | category | flops | bytes accessed | tf_op | source)
XLA Modules:
  0.0 42.0 jit_solution(13445520348834778615)
XLA Ops:
  0.6 37.6 %scan_and_seeds.1 = (bf16[256,2048]{1,0:T(8,128)(2,1)}, bf16[2048,512]{1,0:T(8,128)(2,1)}) custom-call(bf16[256,2048]{1,0:T(8,128)(2,1)} %bitcast.7, bf16[256,256]{1,0:T(8,128)(2,1)} %bitcast.8, f32[32,256]{1,0:T(8,128)} %bitcast.9, f32[32,256]{1,0:T(8,128)} %bitcast.10, bf16[2048,512]{1,0:T(8,128)(2,1)} %rx_hbm.1, bf16[2048,256]{1,0:T(8,128)(2,1)} %rbc_hbm.1, ...), custom_call_target="tpu_custom_call" | custom-call | flops 4000000000 | bytes 8000000 | tf_op jit(solution)/shard_map/scan_and_seeds/pallas_call | solution.py:464
  38.2 0.0 copy-start
  38.3 2.5 %copy.16 = bf16[1,256,2048]{2,1,0:T(8,128)(2,1)} copy(bf16[1,256,2048]{2,1,0:T(8,128)(2,1)} %bitcast.6) | data formatting | bytes 2097152
  40.7 0.0 copy-done
  40.7 1.3 %copy.17 = bf16[2048,512]{1,0:T(8,128)(2,1)} copy(bf16[2048,512]{1,0:T(8,128)(2,1)S(1)} %copy-done) | data formatting | bytes 4194304
Async XLA Ops:
  38.2 2.5 %copy-start = (bf16[2048,512]{1,0:T(8,128)(2,1)S(1)}, bf16[2048,512]{1,0:T(8,128)(2,1)}, u32[]{:S(2)}) copy-start(bf16[2048,512]{1,0:T(8,128)(2,1)} %get-tuple-element.9) | copy-start | bytes 6291460

commit v5 on v4

--- a/solution.py
+++ b/solution.py
@@ -72,7 +72,7 @@
     sizes,
     px_hbm, pbc_hbm, pdt_hbm, pdec_hbm, rx_hbm, rbc_hbm, rdt_hbm, rdec_hbm, pack_hbm, len_hbm, prm_hbm, d_hbm,
     pout_hbm, rout_hbm,
-    pdt_ref, pdec_ref, rdt, rdec_ref, pack_ref, len_ref, prm_ref, d_ref, rrow,
+    pdt_ref, pdec_ref, rdt, rdec_ref, pack_ref, len_ref, prm_ref, d_ref, rrow, rgrown,
     px, pbc, rx, rbc, pv, pt, pe, ptot, pacc, dwide, rv, rt, re, rtot, racc, rdecs,
     abuf, arecv, pbuf, precv, seeds, pout, rout,
     in_sem, out_sem, a_send, a_recv, x_send, x_recv, g_recv, up_send, down_send, tu_send, td_send,
@@ -148,14 +148,15 @@
     loads[0].wait()
     loads[1].wait()
     chunk = min(cols, 512)
-    for t in range(2):
-        rows = slice(t * TILE, (t + 1) * TILE)
-        for start in range(0, cols, chunk):
-            here = slice(start, start + chunk)
-            wide = dot(pt[2 * t + 1].astype(BF16), pe[1, :, here])
-            pv[t, :, here] = (px[rows, here].astype(F32) * wide).astype(BF16)
-            last = dot(pt[2 * t, TILE - 8 :, :].astype(BF16), pe[0, :, here])
-            ptot[t, :, here] = jnp.broadcast_to(last[7:8], (8, chunk))
+    weights = jnp.concatenate([pt[1], pt[3]], axis=0).astype(BF16)
+    lasts = jnp.concatenate([pt[0, TILE - 8 :, :], pt[2, TILE - 8 :, :]], axis=0).astype(BF16)
+    for start in range(0, cols, chunk):
+        here = slice(start, start + chunk)
+        scaled = (px[:, here].astype(F32) * dot(weights, pe[1, :, here])).astype(BF16)
+        last = dot(lasts, pe[0, :, here])
+        for t in range(2):
+            pv[t, :, here] = scaled[t * TILE : (t + 1) * TILE]
+            ptot[t, :, here] = jnp.broadcast_to(last[8 * t + 7 : 8 * t + 8], (8, chunk))
     for s in range(seqs):
         here = slice(s * cb, (s + 1) * cb)
         t0, t1 = ptot[0, 0:1, here], ptot[1, 0:1, here]
@@ -284,19 +285,23 @@
         stack += split(jnp.exp2(gain), 2) + [where_rows]
         stack += [jnp.zeros((TILE - 7 * head_rows - 8, TILE), F32)]
         column = jnp.concatenate(stack, axis=0).T
-        wide = dot(column.astype(BF16), re[1])
-        last = dot(column[TILE - 8 :].astype(BF16), re[0])
+        return column, jnp.log2(dt) - c2
+
+    def prepare_some(step, carry):
+        base = pl.multiple_of(step * together * TILE, TILE)
+        rows = pl.ds(base, together * TILE)
+        made = [prepare(step * together + n) for n in range(together)]
+        narrow = jnp.concatenate([column for column, _ in made], axis=0).astype(BF16)
+        wide = dot(narrow, re[1])
+        grown = dot(narrow, re[0])
         scaled = (rx[rows, :].astype(F32) * wide).astype(BF16)
-        return column, jnp.log2(dt) - c2, scaled, jnp.broadcast_to(last[7:8], (8, cb))
-
-    def prepare_some(step, carry):
-        places = [step * together + n for n in range(together)]
-        made = [prepare(tile) for tile in places]
-        for tile, (column, row_form, scaled, last) in zip(places, made):
+        rgrown[rows, :] = grown
+        rv[pl.ds(step * together + 2, together)] = scaled.reshape(together, TILE, cb)
+        for n, (column, row_form) in enumerate(made):
+            tile = step * together + n
             rt[tile] = column
             rrow[tile] = row_form
-            rv[tile + 2] = scaled
-            rtot[tile + 2] = last
+            rtot[tile + 2] = jnp.broadcast_to(grown[(n + 1) * TILE - 1 : (n + 1) * TILE], (8, cb))
         return carry
 
     def within(tile):
@@ -304,7 +309,7 @@
         rows = pl.ds(base, TILE)
         column = rt[tile]
         x_tile = rx[rows, :]
-        grown = dot(column.astype(BF16), re[0])
+        grown = rgrown[rows, :]
         c_rows = rbc[pl.ds(base + 2 * TILE, TILE), STATE:]
         scores = dot_nt(c_rows, rbc[pl.ds(base, 3 * TILE), :STATE])
         j = iota((TILE, 3 * TILE), 1) - 2 * TILE
@@ -360,19 +365,15 @@
         for s in range(seqs):
             precv[s] = jnp.zeros((STATE, cb), BF16)
 
-    p_outs = []
-    for t in range(2):
-        rows = slice(t * TILE, (t + 1) * TILE)
-        narrow = pt[2 * t].astype(BF16)
-        for s in range(seqs):
-            here = slice(s * cb, (s + 1) * cb)
-            grown = dot(narrow, pe[0, :, here])
-            if t == 1:
-                grown = grown * ptot[0, 0:1, here]
-            carried = grown * dot(pbc[rows, STATE:], precv[s])
-            pout[rows, here] = (pacc[rows, here] + carried).astype(BF16)
-        p_outs.append(pltpu.make_async_copy(pout.at[rows], pout_hbm.at[rows], out_sem.at[tiles + t]))
-        p_outs[-1].start()
+    narrow = jnp.concatenate([pt[0], pt[2]], axis=0).astype(BF16)
+    later = iota((2 * TILE, cb), 0) >= TILE
+    for s in range(seqs):
+        here = slice(s * cb, (s + 1) * cb)
+        grown = dot(narrow, pe[0, :, here]) * jnp.where(later, ptot[0, 0:1, here], 1.0)
+        carried = grown * dot(pbc[:, STATE:], precv[s])
+        pout[:, here] = (pacc[:, here] + carried).astype(BF16)
+    p_outs = [pltpu.make_async_copy(pout, pout_hbm, out_sem.at[tiles])]
+    p_outs[0].start()
 
     for level in range(levels):
         which = level * 2 + 1 - core
@@ -380,33 +381,28 @@
             src_ref=seeds.at[which], dst_ref=seeds.at[which], send_sem=tu_send.at[0], recv_sem=g_recv.at[which],
             device_id={"grp": twin}, device_id_type=MESH).wait_recv()
 
-    def out_copy(tile):
-        rows = pl.ds(pl.multiple_of(tile * TILE, TILE), TILE)
-        return pltpu.make_async_copy(rout.at[rows], rout_hbm.at[rows], out_sem.at[tile])
-
-    def seeded(tile):
-        base = pl.multiple_of(tile * TILE, TILE)
-        column = rt[tile]
+    def out_copy(step):
+        rows = pl.ds(pl.multiple_of(step * together * TILE, TILE), together * TILE)
+        return pltpu.make_async_copy(rout.at[rows], rout_hbm.at[rows], out_sem.at[step])
+
+    def seed_tiles(step, carry):
+        base = pl.multiple_of(step * together * TILE, TILE)
+        rows = pl.ds(base, together * TILE)
+        column = rt[pl.ds(step * together, together)].reshape(together * TILE, TILE)
         owner = column[:, 7 * head_rows + 1 : 7 * head_rows + 2].astype(jnp.int32)
-        c_rows = rbc[pl.ds(base + 2 * TILE, TILE), STATE:].astype(F32)
+        c_rows = rbc[pl.ds(base + 2 * TILE, together * TILE), STATE:].astype(F32)
         batch = 8 if grps % 8 == 0 else 2
-        total = jnp.zeros((TILE, cb), F32)
+        total = jnp.zeros((together * TILE, cb), F32)
         for q in range(0, grps, batch):
-            chosen = [jnp.where(owner == q + n, c_rows, 0.0) for n in range(batch)]
+            chosen = [jnp.where(owner == q + n, c_rows, 0.0).astype(BF16) for n in range(batch)]
             table = seeds[q : q + batch].reshape(batch * STATE, cb)
-            total = total + dot(jnp.concatenate(chosen, axis=1).astype(BF16), table)
-        result = racc[pl.ds(base, TILE), :] + dot(column.astype(BF16), re[2]) * total
-        return jnp.where(owner >= 0, result, 0.0).astype(BF16)
-
-    def seed_tiles(step, carry):
-        places = [step * 2 + n for n in range(2)]
-        made = [seeded(tile) for tile in places]
-        for tile, result in zip(places, made):
-            rout[pl.ds(pl.multiple_of(tile * TILE, TILE), TILE), :] = result
-            out_copy(tile).start()
+            total = total + dot(jnp.concatenate(chosen, axis=1), table)
+        result = racc[rows, :] + dot(column.astype(BF16), re[2]) * total
+        rout[rows, :] = jnp.where(owner >= 0, result, 0.0).astype(BF16)
+        out_copy(step).start()
         return carry
 
-    lax.fori_loop(0, tiles // 2, seed_tiles, 0)
+    lax.fori_loop(0, tiles // together, seed_tiles, 0)
 
     for step in range(1, seqs):
         state_copy(step).wait_send()
@@ -437,11 +433,11 @@
     for copy in p_outs:
         copy.wait()
 
-    def out_wait(tile, carry):
-        out_copy(tile).wait()
+    def out_wait(step, carry):
+        out_copy(step).wait()
         return carry
 
-    lax.fori_loop(0, tiles, out_wait, 0)
+    lax.fori_loop(0, tiles // together, out_wait, 0)
 
 
 def on_device(
@@ -479,6 +475,7 @@
             pltpu.SMEM(resp_prompt.shape, jnp.int32),
             pltpu.VMEM((1, heads), F32),
             pltpu.VMEM((tiles, head_rows, TILE), F32),
+            pltpu.VMEM((tiles * TILE, cb), F32),
             pltpu.VMEM((2 * TILE, cols), BF16),
             pltpu.VMEM((2 * TILE, 2 * STATE), BF16),
             pltpu.VMEM((tiles * TILE, cb), BF16),

time: 42.2 us -> 39.5 us (0.936)
  Pallas kernels: 37.6 us -> 35 us
    pallas_call x1, Pallas kernels: 37.6 us -> 35 us  [on_device(): pl.pallas_call(functools.partial(kernel, sizes), out_shape=(jax.ShapeDtyp...]
where the time goes in v5:
time: 39.5 us; the launch traced here: 39.4 us
  Pallas kernels  35 us (89%)
  local copies, waits for them, and re-layouts  3.78 us (10%)
  between operations  0.65 us (2%)
    pallas_call x1, Pallas kernels, on_device(): pl.pallas_call(functools.partial(kernel, sizes), out_shape=(jax.ShapeDtyp...  35 us
    unnamed x4, local copies, waits for them, and re-layouts  3.78 us

profile of v5, /device:TPU:0, one launch (start us, length us, event | category | flops | bytes accessed | tf_op | source)
XLA Modules:
  0.0 39.4 jit_solution(14441080660302189755)
XLA Ops:
  0.6 35.0 %scan_and_seeds.1 = (bf16[256,2048]{1,0:T(8,128)(2,1)}, bf16[2048,512]{1,0:T(8,128)(2,1)}) custom-call(bf16[256,2048]{1,0:T(8,128)(2,1)} %bitcast.7, bf16[256,256]{1,0:T(8,128)(2,1)} %bitcast.8, f32[32,256]{1,0:T(8,128)} %bitcast.9, f32[32,256]{1,0:T(8,128)} %bitcast.10, bf16[2048,512]{1,0:T(8,128)(2,1)} %rx_hbm.1, bf16[2048,256]{1,0:T(8,128)(2,1)} %rbc_hbm.1, ...), custom_call_target="tpu_custom_call" | custom-call | flops 4000000000 | bytes 8000000 | tf_op jit(solution)/shard_map/scan_and_seeds/pallas_call | solution.py:460
  35.6 0.0 copy-start
  35.6 2.5 %copy.16 = bf16[1,256,2048]{2,1,0:T(8,128)(2,1)} copy(bf16[1,256,2048]{2,1,0:T(8,128)(2,1)} %bitcast.6) | data formatting | bytes 2097152
  38.1 0.0 copy-done
  38.1 1.3 %copy.17 = bf16[2048,512]{1,0:T(8,128)(2,1)} copy(bf16[2048,512]{1,0:T(8,128)(2,1)S(1)} %copy-done) | data formatting | bytes 4194304
Async XLA Ops:
  35.6 2.5 %copy-start = (bf16[2048,512]{1,0:T(8,128)(2,1)S(1)}, bf16[2048,512]{1,0:T(8,128)(2,1)}, u32[]{:S(2)}) copy-start(bf16[2048,512]{1,0:T(8,128)(2,1)} %get-tuple-element.9) | copy-start | bytes 6291460

commit v6 on v5

--- a/solution.py
+++ b/solution.py
@@ -323,7 +323,7 @@
         return jnp.concatenate(pieces, axis=1) + grown * earlier + skip * x_tile.astype(F32)
 
     def response_tiles(step, carry):
-        places = [step * 2 + n for n in range(2)]
+        places = [step * 4 + n for n in range(4)]
         made = [within(tile) for tile in places]
         for tile, total in zip(places, made):
             racc[pl.ds(pl.multiple_of(tile * TILE, TILE), TILE), :] = total
@@ -342,8 +342,8 @@
             pass_on(z + distance, distance, False)
             seed_copy(z + distance, twin, td_send.at[distance]).start()
 
-    together = 4
-    share = tiles // 8
+    together = 8
+    share = tiles // 16
     lax.fori_loop(0, tiles // together, prepare_some, 0)
     relay(1)
     lax.fori_loop(0, share, response_tiles, 0)

time: 39.5 us -> 39.2 us (level)
  Pallas kernels: 35 us -> 34.6 us
where the time goes in v6:
time: 39.2 us; the launch traced here: 39 us
  Pallas kernels  34.6 us (88%)
  local copies, waits for them, and re-layouts  3.78 us (10%)
  between operations  0.65 us (2%)
    pallas_call x1, Pallas kernels, on_device(): pl.pallas_call(functools.partial(kernel, sizes), out_shape=(jax.ShapeDtyp...  34.6 us
    unnamed x4, local copies, waits for them, and re-layouts  3.78 us

profile of v6, /device:TPU:0, one launch (start us, length us, event | category | flops | bytes accessed | tf_op | source)
XLA Modules:
  0.0 39.0 jit_solution(15675384428070820624)
XLA Ops:
  0.6 34.6 %scan_and_seeds.1 = (bf16[256,2048]{1,0:T(8,128)(2,1)}, bf16[2048,512]{1,0:T(8,128)(2,1)}) custom-call(bf16[256,2048]{1,0:T(8,128)(2,1)} %bitcast.7, bf16[256,256]{1,0:T(8,128)(2,1)} %bitcast.8, f32[32,256]{1,0:T(8,128)} %bitcast.9, f32[32,256]{1,0:T(8,128)} %bitcast.10, bf16[2048,512]{1,0:T(8,128)(2,1)} %rx_hbm.1, bf16[2048,256]{1,0:T(8,128)(2,1)} %rbc_hbm.1, ...), custom_call_target="tpu_custom_call" | custom-call | flops 4000000000 | bytes 8000000 | tf_op jit(solution)/shard_map/scan_and_seeds/pallas_call | solution.py:460
  35.3 0.0 copy-start
  35.3 2.5 %copy.16 = bf16[1,256,2048]{2,1,0:T(8,128)(2,1)} copy(bf16[1,256,2048]{2,1,0:T(8,128)(2,1)} %bitcast.6) | data formatting | bytes 2097152
  37.7 0.0 copy-done
  37.7 1.3 %copy.17 = bf16[2048,512]{1,0:T(8,128)(2,1)} copy(bf16[2048,512]{1,0:T(8,128)(2,1)S(1)} %copy-done) | data formatting | bytes 4194304
Async XLA Ops:
  35.3 2.5 %copy-start = (bf16[2048,512]{1,0:T(8,128)(2,1)S(1)}, bf16[2048,512]{1,0:T(8,128)(2,1)}, u32[]{:S(2)}) copy-start(bf16[2048,512]{1,0:T(8,128)(2,1)} %get-tuple-element.9) | copy-start | bytes 6291460
